TPU v7x, 32 devices: a whole 2x2x4 slice. The times are simulated.
32 devices in a mesh: slab: 8 (over z, y), brick: 4 (over x, core).
Axes of the slice: x: 2, y: 2, z: 4, core: 2. Of those that a mesh axis runs over, the one named last changes fastest.
Arguments:
- positions: float32 [2048, 3, 128], P(('slab', 'brick')), may hold values from -6 to 6
- velocities: float32 [2048, 3, 128], P(('slab', 'brick')), may hold values from -6 to 6
- radii: float32 [2048, 128], P(('slab', 'brick')), may hold values from 0.6 to 1.2
- cell_of: int32 [2048, 128], P(('slab', 'brick')), may hold values from 0 to 65535
- block_route: int32 [2048, 1], P(('slab', 'brick')), may hold values from 0 to 11; in each aligned block of 64 rows (0 to 63, 64 to 127, ...) at most 11 rows name the same one
- ghost_list: int32 [512], P(('slab', 'brick')), may hold values from 0 to 63
- tile_home: int32 [4096], P(('slab', 'brick')), may hold values from 0 to 63
- tile_partner: int32 [4096], P(('slab', 'brick')), may hold values from 0 to 95
- fluid: float32 [3, 32, 128, 512], P(None, 'slab', 'brick'), may hold values from -6 to 6
Outputs:
- velocity_next: float32 [2048, 3, 128], P(('slab', 'brick'))
- fluid_next: float32 [3, 32, 128, 512], P(None, 'slab', 'brick')
Inputs may be any that keep to these rules, and one draw needn't show every extreme that they name: `block_route`: within the blocks of one device no code appears more than 11 times, and some device's blocks reach 11 for some code.
All inputs are finite; a program needn't handle non-finite values.
Results may differ from a plain program's by a relative error of at most 0.00013.
Values sent between devices are 32-bit elements; how exact they have to be, the bound alone decides.
No kernel may reach another device: no remote copies, remote signals or barrier semaphores. Data moves between devices by JAX's collectives and lax.ppermute only.
A program may use at most 64 MiB of HBM per device.

v0:
```python
import functools
import math

import jax
import jax.numpy as jnp
from jax import lax
from jax.experimental import pallas as pl
from jax.experimental.pallas import tpu as pltpu
from jax.sharding import PartitionSpec as P

stiffness = 0.01
damping = 0.005
viscosity = 0.1
coupling = 0.5
relaxation = 0.5

f32 = jnp.float32
bf16 = jnp.bfloat16
VMEM = pl.BlockSpec(memory_space=pltpu.VMEM)
SMEM = pl.BlockSpec(memory_space=pltpu.SMEM)
HBM = pl.BlockSpec(memory_space=pltpu.HBM)
UNROLL = 8
GROUP = 4


def rows_up(count):
    return -(-count // 8) * 8


def call(body, outs, ins, scratch, name, flops=0, nbytes=1 << 20, places=None):
    return pl.pallas_call(
        body,
        out_shape=outs,
        in_specs=ins,
        out_specs=places or [VMEM] * len(outs),
        scratch_shapes=scratch,
        name=name,
        compiler_params=pltpu.CompilerParams(vmem_limit_bytes=40 << 20),
        cost_estimate=pl.CostEstimate(flops=flops, bytes_accessed=nbytes, transcendentals=0),
    )


def rounded(x):
    return x.astype(bf16).astype(f32)


def iota(shape, dim):
    return lax.broadcasted_iota(jnp.int32, shape, dim)


planes = 7


def copy_all(pairs, sems):
    copies = [pltpu.make_async_copy(*pair, sems.at[i]) for i, pair in enumerate(pairs)]
    for copy in copies:
        copy.start()
    return copies


def wait_all(copies):
    for copy in copies:
        copy.wait()


def pack_kernel(ghost_ref, state, fluid, up, down, right, left):
    count = ghost_ref.shape[0] // 4
    width = state.shape[2]
    nx, ny, nz = fluid.shape[1:]
    for group in range(4):
        i, j = group // 2, group % 2
        slab_to, brick_to = (up if i else down), (right if j else left)
        for g in range(count):
            block = pl.ds(ghost_ref[group * count + g], 1)
            for c in range(planes):
                row = state[c, block, :]
                at = c * 2 * count + j * count + g
                slab_to[at : at + 1, :] = row
                at = c * 2 * count + i * count + g
                brick_to[at : at + 1, :] = row
    for slab_to, x in ((up, nx - 1), (down, 0)):
        for c in range(3):
            for k in range(nz // width):
                at = planes * 2 * count + (c * (nz // width) + k) * ny
                slab_to[at : at + ny, :] = fluid[c, x, :, k * width : (k + 1) * width]
    for brick_to, y in ((right, ny - 1), (left, 0)):
        for c in range(3):
            for x in range(nx):
                for k in range(nz // width):
                    at = planes * 2 * count + (c * nx + x) * (nz // width) + k
                    brick_to[at : at + 1, :] = fluid[
                        c, x, y : y + 1, k * width : (k + 1) * width
                    ]


def three_parts(x):
    one = rounded(x)
    rest = x - one
    two = rounded(rest)
    return one, two, rest - two


def put_rows(ref, stride, rows):
    count = rows[0].shape[0]
    for k, row in enumerate(rows):
        ref[pl.ds(k, count, stride=stride), :] = row


def pair_factors(place):
    parts = [three_parts(plane) for plane in place]
    own = three_parts(
        place[3] * place[3] - place[0] * place[0] - place[1] * place[1] - place[2] * place[2]
    )
    return [[part[k] for part in parts] for k in range(3)], list(own)


def home_rows(place):
    (one, two, three), own = pair_factors(place)
    ones, zeros = jnp.ones_like(place[0]), jnp.zeros_like(place[0])
    rows = one + one + two + two + one + three
    return [2.0 * row for row in rows] + own + [ones] * 3 + [zeros] * 2


def partner_rows(place):
    (one, two, three), own = pair_factors(place)
    ones, zeros = jnp.ones_like(place[0]), jnp.zeros_like(place[0])
    return one + two + one + two + three + one + [ones] * 3 + own + [zeros] * 2


def value_rows(values):
    highs = [rounded(plane) for plane in values]
    ones, zeros = jnp.ones_like(values[0]), jnp.zeros_like(values[0])
    lows = [plane - high for plane, high in zip(values, highs)]
    return highs + [ones, zeros] + lows + [zeros, zeros]


def prepare_partners(place, speeds, rows, columns, values):
    count, width = place[0].shape
    put_rows(rows, 32, partner_rows(place))
    put_rows(values, 16, value_rows(place[0:3] + speeds))

    def turn(b, _):
        block = rows[pl.ds(pl.multiple_of(b * 32, 32), 32), :]
        columns[b] = jnp.transpose(block).astype(bf16)
        return 0

    lax.fori_loop(0, count, turn, 0, unroll=4)


def list_tiles(home_ref, partner_ref, homes, partners, lower, upper, spare):
    def one(t, count):
        partner = partner_ref[t]
        homes[count] = home_ref[t]
        partners[count] = partner - lower
        return count + jnp.where((partner >= lower) & (partner < upper), 1, 0)

    count = lax.fori_loop(0, home_ref.shape[0], one, 0, unroll=4)
    for pad in range(UNROLL):
        homes[count + pad] = spare
        partners[count + pad] = 0
    return count


def add_tiles(count, homes, partners, home_side, partner_side, values, sums):
    def some(step, _):
        for k in range(UNROLL):
            home = homes[step * UNROLL + k]
            partner = partners[step * UNROLL + k]
            factors = home_side[pl.ds(pl.multiple_of(home * 32, 32), 32), :].astype(bf16)
            weight = jnp.dot(partner_side[partner], factors, preferred_element_type=f32)
            weight = jnp.maximum(weight, 0.0)
            high = weight.astype(bf16)
            low = (weight - high.astype(f32)).astype(bf16)
            value = values[pl.ds(pl.multiple_of(partner * 16, 16), 16), :].astype(bf16)
            at = pl.ds(pl.multiple_of(home * 16, 16), 16)
            sums[at, :] += jnp.dot(
                jnp.concatenate([value, value], axis=1),
                jnp.concatenate([high, low], axis=0),
                preferred_element_type=f32,
            )
        return 0

    lax.fori_loop(0, (count + UNROLL - 1) // UNROLL, some, 0)


def own_contacts(home_list, partner_list, state, home_side, sums,
                 rows, columns, values, homes, partners, home_ref, partner_ref, sems):
    nblocks, width = state.shape[1:]
    copies = copy_all([(home_list, home_ref), (partner_list, partner_ref)], sems)
    place = [state[c] for c in range(4)]
    put_rows(home_side, 32, home_rows(place))
    prepare_partners(place, [state[c] for c in (4, 5, 6)], rows, columns, values)
    home_side[nblocks * 32 :, :] = jnp.zeros((32, width), f32)
    sums[...] = jnp.zeros(sums.shape, f32)
    wait_all(copies)
    count = list_tiles(home_ref, partner_ref, homes, partners, 0, nblocks, nblocks)
    add_tiles(count, homes, partners, home_side, columns, values, sums)


def diffuse(fluid, below, above, before, after, skip, diffused):
    nx, ny, nz = fluid.shape[1:]
    width = before.shape[1]
    deep = iota((ny, nz), 1)

    def face(ref, c, x):
        at = skip + (c * nx + x) * (nz // width)
        return jnp.concatenate(
            [ref[at + k : at + k + 1, :] for k in range(nz // width)], axis=1
        )

    def layer(ref, c):
        at = [skip + (c * (nz // width) + k) * ny for k in range(nz // width)]
        return jnp.concatenate([ref[start : start + ny, :] for start in at], axis=1)

    for x in range(nx):
        for c in range(3):
            here = fluid[c, x]
            near = (layer(below, c) if x == 0 else fluid[c, x - 1]) + (
                layer(above, c) if x == nx - 1 else fluid[c, x + 1]
            )
            near = near + jnp.concatenate([face(before, c, x), here[:-1]], axis=0)
            near = near + jnp.concatenate([here[1:], face(after, c, x)], axis=0)
            near = near + jnp.where(deep == 0, 0.0, pltpu.roll(here, 1, 1))
            near = near + jnp.where(deep == nz - 1, 0.0, pltpu.roll(here, nz - 1, 1))
            diffused[c, x] = here + viscosity * (near - 6.0 * here)


def ghost_contacts(nbrick, cap, partner_blocks, home_list, partner_list, routes, below, above, before, after,
                   home_side, own_sums, state, fluid,
                   updated, outgoing, diffused,
                   rows, columns, values, sums, homes, partners, taken,
                   home_ref, partner_ref, route_ref, flow, sems):
    nblocks, width = state.shape[1:]
    per = partner_blocks // 4
    copies = copy_all(
        [
            (home_list, home_ref),
            (partner_list, partner_ref),
            (routes, route_ref),
            (fluid, flow),
        ],
        sems,
    )
    stacked = [
        jnp.concatenate(
            [ref[c * per : (c + 1) * per, :] for ref in (below, above, before, after)], axis=0
        )
        for c in range(planes)
    ]
    prepare_partners(stacked[0:4], stacked[4:7], rows, columns, values)
    sums[...] = own_sums[...]
    wait_all(copies)
    count = list_tiles(home_ref, partner_ref, homes, partners, nblocks, nblocks + 4 * per, nblocks)
    add_tiles(count, homes, partners, home_side, columns, values, sums)
    diffuse(flow, below, above, before, after, planes * per, diffused)

    def total(k):
        high = sums[pl.ds(k, nblocks, stride=16), :]
        return high + sums[pl.ds(k + 8, nblocks, stride=16), :]

    weights = total(6)
    radius = state[3]
    inverse = 1.0 / (radius * radius * radius)
    for c in range(3):
        speed = state[c + 4]
        spring = state[c] * weights - total(c)
        friction = total(c + 3) - speed * weights
        updated[c] = speed + (stiffness * spring + damping * friction) * inverse

    chunk = rows_up(5 * cap + 1)
    for code in range(3 * nbrick):
        taken[code] = 0

    def send(b, _):
        code = route_ref[b]
        spot = taken[code]
        taken[code] = spot + 1
        row = ((code % nbrick) * 3 + code // nbrick) * chunk + spot
        outgoing[pl.ds(row, 1), :] = state[3, pl.ds(b, 1), :]
        for c in range(3):
            outgoing[pl.ds(row + (c + 1) * cap, 1), :] = updated[c, pl.ds(b, 1), :]
        outgoing[pl.ds(row + 4 * cap, 1), :] = state[planes, pl.ds(b, 1), :]
        return 0

    lax.fori_loop(0, nblocks, send, 0, unroll=4)
    for code in range(3 * nbrick):
        row = ((code % nbrick) * 3 + code // nbrick) * chunk + 5 * cap
        outgoing[row : row + 1, :] = jnp.full((1, width), taken[code], jnp.int32).astype(f32)


def list_blocks(arrived, starts, ends, cap, places):
    base, goal = places
    count = 0
    for start, end in zip(starts, ends):
        here = jnp.max(arrived[start + 5 * cap : start + 5 * cap + 1, :]).astype(jnp.int32)
        for spot in range(cap):
            base[count] = start + spot
            goal[count] = end + spot
            count = count + jnp.where(spot < here, 1, 0)
    for pad in range(GROUP):
        base[count + pad] = base[jnp.maximum(count - 1, 0)]
        goal[count + pad] = goal[jnp.maximum(count - 1, 0)]
    return count


def cell_parts(arrived, row, cap, depth):
    cell = arrived[pl.ds(row + 4 * cap, 1), :].astype(jnp.int32)
    shift = depth.bit_length() - 1
    return cell >> shift, cell & (depth - 1)


def level_hot(level, depth):
    width = level.shape[1]
    return jnp.where(iota((depth, width), 0) == level, 1.0, 0.0).astype(bf16)


def deposit(count, arrived, places, cap, total):
    columns, depth = total.shape[0] // 4, total.shape[1]
    width = arrived.shape[1]

    def some(step, _):
        loads_of, levels_of = [], []
        for k in range(GROUP):
            index = step * GROUP + k
            row = places[0][index]
            column, level = cell_parts(arrived, row, cap, depth)
            radius = arrived[pl.ds(row, 1), :]
            mass = radius * radius * radius * jnp.where(index < count, 1.0, 0.0)
            loads = [mass] + [mass * arrived[pl.ds(row + c * cap, 1), :] for c in (1, 2, 3)]
            hit = iota((columns, width), 0) == column
            highs, lows = [], []
            for load in loads:
                high = rounded(load)
                highs.append(jnp.where(hit, high, 0.0).astype(bf16))
                lows.append(jnp.where(hit, load - high, 0.0).astype(bf16))
            hot = level_hot(level, depth)
            loads_of += [jnp.concatenate(highs, axis=0), jnp.concatenate(lows, axis=0)]
            levels_of += [hot, hot]
        total[...] += lax.dot_general(
            jnp.concatenate(loads_of, axis=1),
            jnp.concatenate(levels_of, axis=1),
            (((1,), (1,)), ((), ())),
            preferred_element_type=f32,
        )
        return 0

    lax.fori_loop(0, (count + GROUP - 1) // GROUP, some, 0)


def sample(count, arrived, places, cap, table, answers):
    depth = table.shape[1]
    columns = table.shape[0] // 6
    width = arrived.shape[1]

    def some(step, _):
        hots, hits = [], []
        for k in range(GROUP):
            column, level = cell_parts(arrived, places[0][step * GROUP + k], cap, depth)
            hots.append(level_hot(level, depth))
            hits.append(iota((columns, width), 0) == column)
        along = jnp.dot(table[...], jnp.concatenate(hots, axis=1), preferred_element_type=f32)
        for k in range(GROUP):
            goal = places[1][step * GROUP + k]
            part = along[:, k * width : (k + 1) * width]
            for c in range(3):
                value = part[c * columns : (c + 1) * columns]
                value = value + part[(c + 3) * columns : (c + 4) * columns]
                found = jnp.sum(jnp.where(hits[k], value, 0.0), axis=0, keepdims=True)
                answers[pl.ds(goal + c * cap, 1), :] = found
        return 0

    lax.fori_loop(0, (count + GROUP - 1) // GROUP, some, 0)


def first_deposit(nbrick, cap, crossed, total, base, goal):
    chunk = rows_up(5 * cap + 1)
    total[...] = jnp.zeros(total.shape, f32)
    starts = [(3 * b + 1) * chunk for b in range(nbrick)]
    count = list_blocks(crossed, starts, starts, cap, (base, goal))
    deposit(count, crossed, (base, goal), cap, total)


def advance(nbrick, cap, above, below, start, fluid, diffused, fluid_next, table, answers_up,
            answers_down, arrived, answers, total, flow, fresh_flow, base, goal, sems):
    reading = pltpu.make_async_copy(fluid, flow, sems.at[0])
    reading.start()
    chunk = rows_up(5 * cap + 1)
    back = rows_up(3 * cap)
    rows = nbrick * chunk
    arrived[0:rows, :] = above[...]
    arrived[rows:, :] = below[...]
    starts = [i * chunk for i in range(2 * nbrick)]
    ends = [i * back for i in range(2 * nbrick)]
    total[...] = start[...]
    count = list_blocks(arrived, starts, ends, cap, (base, goal))
    deposit(count, arrived, (base, goal), cap, total)
    reading.wait()

    nx, ny, nz = flow.shape[1:]
    columns = nx * ny
    for x in range(nx):
        volume = total[x * ny : (x + 1) * ny, :]
        for c in range(3):
            at = (c + 1) * columns + x * ny
            moved = total[at : at + ny, :] - volume * flow[c, x]
            fresh = diffused[c, x] + coupling * moved
            fresh_flow[c, x] = fresh
            high = fresh.astype(bf16)
            at = c * columns + x * ny
            table[at : at + ny, :] = high
            table[at + 3 * columns : at + 3 * columns + ny, :] = (
                fresh - high.astype(f32)
            ).astype(bf16)
    writing = pltpu.make_async_copy(fresh_flow, fluid_next, sems.at[1])
    writing.start()
    sample(count, arrived, (base, goal), cap, table, answers)
    answers_up[...] = answers[0 : nbrick * back, :]
    answers_down[...] = answers[nbrick * back :, :]
    writing.wait()


def last_sample(nbrick, cap, crossed, table, answers, base, goal):
    chunk = rows_up(5 * cap + 1)
    back = rows_up(3 * cap)
    starts = [(3 * b + 1) * chunk for b in range(nbrick)]
    ends = [b * back for b in range(nbrick)]
    count = list_blocks(crossed, starts, ends, cap, (base, goal))
    sample(count, crossed, (base, goal), cap, table, answers)


def relax(nbrick, cap, route_ref, updated, returned, velocity_next, picked, taken):
    back = rows_up(3 * cap)
    for code in range(3 * nbrick):
        taken[code] = 0

    def one(b, _):
        code = route_ref[b]
        spot = taken[code]
        taken[code] = spot + 1
        row = ((code % nbrick) * 3 + code // nbrick) * back + spot
        for c in range(3):
            picked[c, pl.ds(b, 1), :] = returned[pl.ds(row + c * cap, 1), :]
        return 0

    lax.fori_loop(0, updated.shape[1], one, 0, unroll=4)
    now = updated[...]
    velocity_next[...] = now + relaxation * (picked[...] - now)


def on_device(
    positions, velocities, radii, cell_of, block_route, ghost_list, tile_home, tile_partner, fluid
):
    nblocks, _, width = positions.shape
    nbrick = lax.axis_size("brick")
    _, nx, ny, nz = fluid.shape
    columns = nx * ny
    codes = 3 * nbrick
    cap = max(2, (2 * nblocks + codes - 1) // codes)
    chunk, back = rows_up(5 * cap + 1), rows_up(3 * cap)
    per = ghost_list.shape[0] // 2
    tiles = tile_home.shape[0]
    routes = block_route.reshape(-1)
    positions = jnp.transpose(positions, (1, 0, 2))
    velocities = jnp.transpose(velocities, (1, 0, 2))

    def struct(*shape, dtype=f32):
        return jax.ShapeDtypeStruct(shape, dtype)

    def shifted(x, axis, step):
        count = lax.axis_size(axis)
        return lax.ppermute(x, axis, [(i, (i + step) % count) for i in range(count)])

    def ints(count):
        return pltpu.SMEM((count,), jnp.int32)

    state = jnp.concatenate(
        [positions, radii[None], velocities, cell_of.astype(f32)[None]], axis=0
    )
    ghost_rows, chunks = planes * per, 3 * (nz // width)
    up, down, right, left = call(
        pack_kernel,
        [struct(ghost_rows + chunks * ny, width)] * 2 + [struct(ghost_rows + chunks * nx, width)] * 2,
        [SMEM] + [VMEM] * 2,
        [],
        "pack",
    )(ghost_list, state, fluid)
    below = shifted(up, "slab", 1)
    above = shifted(down, "slab", -1)
    before = shifted(right, "brick", 1)
    after = shifted(left, "brick", -1)

    def sides(count):
        return [
            pltpu.VMEM((count * 32, width), f32),
            pltpu.VMEM((count, width, 32), bf16),
            pltpu.VMEM((count * 16, width), f32),
        ]

    lists = [ints(tiles + UNROLL)] * 2
    contact_flops = tiles * width * width * 200
    home_side, sums = call(
        own_contacts,
        [struct((nblocks + 1) * 32, width), struct((nblocks + 1) * 16, width)],
        [HBM] * 2 + [VMEM],
        sides(nblocks) + lists + [ints(tiles)] * 2 + [pltpu.SemaphoreType.DMA((2,))],
        "own_contacts",
        contact_flops,
    )(tile_home, tile_partner, state)
    updated, outgoing, diffused = call(
        functools.partial(ghost_contacts, nbrick, cap, 4 * per),
        [struct(3, nblocks, width), struct(nbrick * 3 * chunk, width), struct(3, nx, ny, nz)],
        [HBM] * 3 + [VMEM] * 7 + [HBM],
        sides(4 * per)
        + [pltpu.VMEM(((nblocks + 1) * 16, width), f32)]
        + lists
        + [ints(codes), ints(tiles), ints(tiles), ints(nblocks)]
        + [pltpu.VMEM((3, nx, ny, nz), f32), pltpu.SemaphoreType.DMA((4,))],
        "ghost_contacts",
        contact_flops // 2,
    )(tile_home, tile_partner, routes, below, above, before, after,
      home_side, sums, state, fluid)

    crossed = lax.all_to_all(
        outgoing.reshape(nbrick, 3 * chunk, width), "brick", split_axis=0, concat_axis=0, tiled=True
    )
    from_above = shifted(crossed[:, 0:chunk], "slab", -1).reshape(nbrick * chunk, width)
    from_below = shifted(crossed[:, 2 * chunk :], "slab", 1).reshape(nbrick * chunk, width)
    crossed = crossed.reshape(nbrick * 3 * chunk, width)

    def places(count):
        return [ints(count + GROUP)] * 2

    block_flops = 16 * columns * nz * width
    (started,) = call(
        functools.partial(first_deposit, nbrick, cap),
        [struct(4 * columns, nz)],
        [VMEM],
        places(nbrick * cap),
        "first_deposit",
        block_flops * nblocks // 3,
    )(crossed)
    fluid_next, table, answers_up, answers_down = call(
        functools.partial(advance, nbrick, cap),
        [
            struct(3, nx, ny, nz),
            struct(6 * columns, nz, dtype=bf16),
            struct(nbrick * back, width),
            struct(nbrick * back, width),
        ],
        [VMEM] * 3 + [HBM, VMEM],
        [
            pltpu.VMEM((2 * nbrick * chunk, width), f32),
            pltpu.VMEM((2 * nbrick * back, width), f32),
            pltpu.VMEM((4 * columns, nz), f32),
        ]
        + [pltpu.VMEM((3, nx, ny, nz), f32)] * 2
        + places(2 * nbrick * cap)
        + [pltpu.SemaphoreType.DMA((2,))],
        "advance",
        block_flops * nblocks,
        places=[HBM] + [VMEM] * 3,
    )(from_above, from_below, started, fluid, diffused)
    answers_up = shifted(answers_up.reshape(nbrick, back, width), "slab", 1)
    answers_down = shifted(answers_down.reshape(nbrick, back, width), "slab", -1)
    (answers,) = call(
        functools.partial(last_sample, nbrick, cap),
        [struct(nbrick * back, width)],
        [VMEM] * 2,
        places(nbrick * cap),
        "last_sample",
        block_flops * nblocks // 4,
    )(crossed, table)
    answers = jnp.concatenate(
        [answers_up, answers.reshape(nbrick, back, width), answers_down], axis=1
    )
    returned = lax.all_to_all(answers, "brick", split_axis=0, concat_axis=0, tiled=True)
    (velocity_next,) = call(
        functools.partial(relax, nbrick, cap),
        [struct(3, nblocks, width)],
        [SMEM] + [VMEM] * 2,
        [pltpu.VMEM((3, nblocks, width), f32), ints(codes)],
        "relax",
    )(routes, updated, returned.reshape(nbrick * 3 * back, width))
    return (jnp.transpose(velocity_next, (1, 0, 2)), fluid_next)


def solution(mesh):
    placed = (
        P(("slab", "brick"), None, None),
        P(("slab", "brick"), None, None),
        P(("slab", "brick"), None),
        P(("slab", "brick"), None),
        P(("slab", "brick"), None),
        P(("slab", "brick")),
        P(("slab", "brick")),
        P(("slab", "brick")),
        P(None, "slab", "brick", None),
    )
    return jax.shard_map(
        on_device,
        mesh=mesh,
        in_specs=placed,
        out_specs=(P(("slab", "brick"), None, None), P(None, "slab", "brick", None)),
        check_vma=False,
    )
```

profile of v0, /device:TPU:0, one launch (start us, length us, event | category | flops | bytes accessed | tf_op | source)
XLA Modules:
  0.0 87.5 jit_solution(2715739266462343209)
XLA Ops:
  0.7 0.8 convert_bitcast_fusion
  1.4 1.0 %pad_maximum_fusion.state = f32[8,64,128]{2,1,0:T(8,128)S(1)} fusion(f32[1,64,128]{2,1,0:T(8,128)S(1)} %convert_bitcast_fusion, f32[3,64,128]{2,1,0:T(8,128)} %bitcast.26, f32[1,64,128]{2,1,0:T(8,128)} %bitcast.29, f32[3,64,128]{2,1,0:T(8,128)} %bitcast.27), kind=kLoop, calls=%fused_computation | loop fusion | flops 196608 | bytes 524288 | tf_op jit(solution)/shard_map/concatenate | solution.py:476
  2.4 0.0 copy-start
  2.4 1.1 %copy-done = f32[3,4,32,512]{3,2,1,0:T(8,128)S(1)} copy-done((f32[3,4,32,512]{3,2,1,0:T(8,128)S(1)}, f32[3,4,32,512]{3,2,1,0:T(8,128)}, u32[]{:S(2)}) %copy-start) | copy-done | bytes 786456
  3.5 0.7 copy-done.3
  4.2 0.7 pack.1
  4.9 3.0 %collective-permute-start = (f32[440,128]{1,0:T(8,128)S(1)}, f32[440,128]{1,0:T(8,128)S(1)}, u32[]{:S(2)}, u32[]{:S(2)}) collective-permute-start(f32[440,128]{1,0:T(8,128)S(1)} %get-tuple-element.15), channel_id=1, source_target_pairs={{0,4},{4,8},{8,12},{12,16},{16,20},{20,24},{24,28},{28,0},{1,5},{5... | collective-permute-start | bytes 675848 | tf_op jit(solution)/shard_map/ppermute | solution.py:471
  7.9 3.1 %collective-permute-start.1 = (f32[440,128]{1,0:T(8,128)S(1)}, f32[440,128]{1,0:T(8,128)S(1)}, u32[]{:S(2)}, u32[]{:S(2)}) collective-permute-start(f32[440,128]{1,0:T(8,128)S(1)} %get-tuple-element.16), channel_id=1, source_target_pairs={{0,28},{4,0},{8,4},{12,8},{16,12},{20,16},{24,20},{28,24},{1,29},{... | collective-permute-start | bytes 675848 | tf_op jit(solution)/shard_map/ppermute | solution.py:471
  11.0 0.0 collective-permute-start.2
  11.0 1.7 %collective-permute-start.3 = (f32[104,128]{1,0:T(8,128)S(1)}, f32[104,128]{1,0:T(8,128)S(1)}, u32[]{:S(2)}, u32[]{:S(2)}) collective-permute-start(f32[104,128]{1,0:T(8,128)S(1)} %get-tuple-element.18), channel_id=1, source_target_pairs={{0,3},{1,0},{2,1},{3,2},{4,7},{5,4},{6,5},{7,6},{8,11},{9,8},{10,9... | collective-permute-start | bytes 159752 | tf_op jit(solution)/shard_map/ppermute | solution.py:471
  12.7 8.3 %own_contacts.1 = (f32[2080,128]{1,0:T(8,128)S(1)}, f32[1040,128]{1,0:T(8,128)S(1)}) custom-call(s32[128]{0:T(128)S(1)} %copy-done.4, s32[128]{0:T(128)S(1)} %copy-done.5, f32[8,64,128]{2,1,0:T(8,128)S(1)} %pad_maximum_fusion.state), custom_call_target="tpu_custom_call" | custom-call | flops 419430400 | bytes 1048576 | tf_op jit(solution)/shard_map/own_contacts/pallas_call | solution.py:501
  21.1 0.0 collective-permute-done.below
  21.1 5.7 %ghost_contacts.1 = (f32[3,64,128]{2,1,0:T(8,128)S(1)}, f32[672,128]{1,0:T(8,128)S(1)}, f32[3,4,32,512]{3,2,1,0:T(8,128)S(1)}) custom-call(s32[128]{0:T(128)S(1)} %copy-done.4, s32[128]{0:T(128)S(1)} %copy-done.5, s32[64]{0:T(128)S(1)} %bitcast.20, f32[440,128]{1,0:T(8,128)S(1)} %collective-permute-done.below, f32[440,128]{1,0:T(8,128)S(1)} %collective-permute-done.1.above, ...), custom_call_target="tpu_custom_call" | custom-call | flops 209715200 | bytes 1048576 | tf_op jit(solution)/shard_map/ghost_contacts/pallas_call | solution.py:509
  26.9 9.6 %all_to_all.10 = f32[4,168,128]{2,1,0:T(8,128)S(1)} all-to-all(f32[4,168,128]{2,1,0:T(8,128)S(1)} %bitcast.18), channel_id=1, replica_groups=mesh['slab'=8,'brick'=4] {'brick'}, dimensions={0} | all-to-all | bytes 688128 | tf_op jit(solution)/shard_map/all_to_all | solution.py:523
  36.5 0.1 collective-permute-start.5
  36.5 4.7 %collective-permute-start.4 = (f32[4,56,128]{2,1,0:T(8,128)S(1)}, f32[4,56,128]{2,1,0:T(8,128)S(1)}, u32[]{:S(2)}, u32[]{:S(2)}) collective-permute-start(f32[4,56,128]{2,1,0:T(8,128)S(1)} %get-tuple-element.29), channel_id=1, source_target_pairs={{0,28},{4,0},{8,4},{12,8},{16,12},{20,16},{24,20},{28,24},{1,29},{... | collective-permute-start | bytes 344072 | tf_op jit(solution)/shard_map/ppermute | solution.py:471
  41.2 8.6 %first_deposit.1.start = f32[512,512]{1,0:T(8,128)S(1)} custom-call(f32[672,128]{1,0:T(8,128)S(1)} %bitcast.16), custom_call_target="tpu_custom_call" | custom-call | flops 2863311616 | bytes 1048576 | tf_op jit(solution)/shard_map/first_deposit/pallas_call | solution.py:534
  49.8 0.0 collective-permute-done.5
  49.8 12.9 %advance.1 = (f32[3,4,32,512]{3,2,1,0:T(8,128)}, bf16[768,512]{1,0:T(8,128)(2,1)S(1)}, f32[160,128]{1,0:T(8,128)S(1)}, f32[160,128]{1,0:T(8,128)S(1)}) custom-call(f32[224,128]{1,0:T(8,128)S(1)} %bitcast.23, f32[224,128]{1,0:T(8,128)S(1)} %bitcast.22, f32[512,512]{1,0:T(8,128)S(1)} %first_deposit.1.start, f32[3,4,32,512]{3,2,1,0:T(8,128)S(1)} %copy-done.1, ...), custom_call_target="tpu_custom_call" | custom-call | flops 8589934592 | bytes 1048576 | tf_op jit(solution)/shard_map/advance/pallas_call | solution.py:542
  62.7 0.1 collective-permute-start.6
  62.8 4.7 %collective-permute-start.7 = (f32[4,40,128]{2,1,0:T(8,128)S(1)}, f32[4,40,128]{2,1,0:T(8,128)S(1)}, u32[]{:S(2)}, u32[]{:S(2)}) collective-permute-start(f32[4,40,128]{2,1,0:T(8,128)S(1)} %bitcast.24), channel_id=1, source_target_pairs={{0,28},{4,0},{8,4},{12,8},{16,12},{20,16},{24,20},{28,24},{1,29},{... | collective-permute-start | bytes 245768 | tf_op jit(solution)/shard_map/ppermute | solution.py:471
  67.5 6.8 %last_sample.1 = f32[160,128]{1,0:T(8,128)S(1)} custom-call(f32[672,128]{1,0:T(8,128)S(1)} %bitcast.17, bf16[768,512]{1,0:T(8,128)(2,1)S(1)} %get-tuple-element.25.table), custom_call_target="tpu_custom_call" | custom-call | flops 2147483648 | bytes 1048576 | tf_op jit(solution)/shard_map/last_sample/pallas_call | solution.py:565
  74.3 11.3 %all_to_all.11 = f32[4,120,128]{2,1,0:T(8,128)S(1)} all-to-all(f32[4,120,128]{2,1,0:T(8,128)S(1)} %pad_maximum_fusion.1), channel_id=1, replica_groups=mesh['slab'=8,'brick'=4] {'brick'}, dimensions={0} | all-to-all | bytes 491520 | tf_op jit(solution)/shard_map/all_to_all | solution.py:576
  85.6 1.9 %relax.1 = f32[3,64,128]{2,1,0:T(8,128)} custom-call(s32[64]{0:T(128)S(1)} %bitcast.21, f32[3,64,128]{2,1,0:T(8,128)S(1)} %get-tuple-element.21.updated, f32[480,128]{1,0:T(8,128)S(1)} %bitcast.15), custom_call_target="tpu_custom_call" | custom-call | bytes 1048576 | tf_op jit(solution)/shard_map/relax/pallas_call | solution.py:577
  (17 shorter events, 0.1 us)
Async XLA Ops:
  0.6 12.1 %copy-start.5 = (s32[128]{0:T(128)S(1)}, s32[128]{0:T(128)}, u32[]{:S(2)}) copy-start(s32[128]{0:T(128)} %partner_list.3) | copy-start | bytes 1540
  0.6 12.1 %copy-start.4 = (s32[128]{0:T(128)S(1)}, s32[128]{0:T(128)}, u32[]{:S(2)}) copy-start(s32[128]{0:T(128)} %home_list.3) | copy-start | bytes 1540
  2.4 1.1 %copy-start = (f32[3,4,32,512]{3,2,1,0:T(8,128)S(1)}, f32[3,4,32,512]{3,2,1,0:T(8,128)}, u32[]{:S(2)}) copy-start(f32[3,4,32,512]{3,2,1,0:T(8,128)} %fluid.5) | copy-start | bytes 2359300
  3.5 0.7 copy-start.3
  4.2 16.9 %copy-start.1 = (f32[3,4,32,512]{3,2,1,0:T(8,128)S(1)}, f32[3,4,32,512]{3,2,1,0:T(8,128)}, u32[]{:S(2)}) copy-start(f32[3,4,32,512]{3,2,1,0:T(8,128)} %fluid.5) | copy-start | bytes 2359300
  4.2 16.9 %copy-start.2 = (s32[64,1]{0,1:T(1,128)S(1)}, s32[64,1]{0,1:T(1,128)}, u32[]{:S(2)}) copy-start(s32[64,1]{0,1:T(1,128)} %param.13) | copy-start | bytes 772
  4.9 16.2 %collective-permute-start = (f32[440,128]{1,0:T(8,128)S(1)}, f32[440,128]{1,0:T(8,128)S(1)}, u32[]{:S(2)}, u32[]{:S(2)}) collective-permute-start(f32[440,128]{1,0:T(8,128)S(1)} %get-tuple-element.15), channel_id=1, source_target_pairs={{0,4},{4,8},{8,12},{12,16},{16,20},{20,24},{24,28},{28,0},{1,5},{5... | collective-permute-start | bytes 675848 | tf_op jit(solution)/shard_map/ppermute | solution.py:471
  7.9 13.2 %collective-permute-start.1 = (f32[440,128]{1,0:T(8,128)S(1)}, f32[440,128]{1,0:T(8,128)S(1)}, u32[]{:S(2)}, u32[]{:S(2)}) collective-permute-start(f32[440,128]{1,0:T(8,128)S(1)} %get-tuple-element.16), channel_id=1, source_target_pairs={{0,28},{4,0},{8,4},{12,8},{16,12},{20,16},{24,20},{28,24},{1,29},{... | collective-permute-start | bytes 675848 | tf_op jit(solution)/shard_map/ppermute | solution.py:471
  11.0 10.1 %collective-permute-start.2 = (f32[104,128]{1,0:T(8,128)S(1)}, f32[104,128]{1,0:T(8,128)S(1)}, u32[]{:S(2)}, u32[]{:S(2)}) collective-permute-start(f32[104,128]{1,0:T(8,128)S(1)} %get-tuple-element.17), channel_id=1, source_target_pairs={{0,1},{1,2},{2,3},{3,0},{4,5},{5,6},{6,7},{7,4},{8,9},{9,10},{10,1... | collective-permute-start | bytes 159752 | tf_op jit(solution)/shard_map/ppermute | solution.py:471
  11.0 10.1 %collective-permute-start.3 = (f32[104,128]{1,0:T(8,128)S(1)}, f32[104,128]{1,0:T(8,128)S(1)}, u32[]{:S(2)}, u32[]{:S(2)}) collective-permute-start(f32[104,128]{1,0:T(8,128)S(1)} %get-tuple-element.18), channel_id=1, source_target_pairs={{0,3},{1,0},{2,1},{3,2},{4,7},{5,4},{6,5},{7,6},{8,11},{9,8},{10,9... | collective-permute-start | bytes 159752 | tf_op jit(solution)/shard_map/ppermute | solution.py:471
  36.5 13.3 %collective-permute-start.5 = (f32[4,56,128]{2,1,0:T(8,128)S(1)}, f32[4,56,128]{2,1,0:T(8,128)S(1)}, u32[]{:S(2)}, u32[]{:S(2)}) collective-permute-start(f32[4,56,128]{2,1,0:T(8,128)S(1)} %get-tuple-element.28), channel_id=1, source_target_pairs={{0,4},{4,8},{8,12},{12,16},{16,20},{20,24},{24,28},{28,0},{1,5},{5... | collective-permute-start | bytes 344072 | tf_op jit(solution)/shard_map/ppermute | solution.py:471
  36.5 13.3 %collective-permute-start.4 = (f32[4,56,128]{2,1,0:T(8,128)S(1)}, f32[4,56,128]{2,1,0:T(8,128)S(1)}, u32[]{:S(2)}, u32[]{:S(2)}) collective-permute-start(f32[4,56,128]{2,1,0:T(8,128)S(1)} %get-tuple-element.29), channel_id=1, source_target_pairs={{0,28},{4,0},{8,4},{12,8},{16,12},{20,16},{24,20},{28,24},{1,29},{... | collective-permute-start | bytes 344072 | tf_op jit(solution)/shard_map/ppermute | solution.py:471
  62.7 11.5 %collective-permute-start.6 = (f32[4,40,128]{2,1,0:T(8,128)S(1)}, f32[4,40,128]{2,1,0:T(8,128)S(1)}, u32[]{:S(2)}, u32[]{:S(2)}) collective-permute-start(f32[4,40,128]{2,1,0:T(8,128)S(1)} %bitcast.25), channel_id=1, source_target_pairs={{0,4},{4,8},{8,12},{12,16},{16,20},{20,24},{24,28},{28,0},{1,5},{5... | collective-permute-start | bytes 245768 | tf_op jit(solution)/shard_map/ppermute | solution.py:471
  62.8 11.5 %collective-permute-start.7 = (f32[4,40,128]{2,1,0:T(8,128)S(1)}, f32[4,40,128]{2,1,0:T(8,128)S(1)}, u32[]{:S(2)}, u32[]{:S(2)}) collective-permute-start(f32[4,40,128]{2,1,0:T(8,128)S(1)} %bitcast.24), channel_id=1, source_target_pairs={{0,28},{4,0},{8,4},{12,8},{16,12},{20,16},{24,20},{28,24},{1,29},{... | collective-permute-start | bytes 245768 | tf_op jit(solution)/shard_map/ppermute | solution.py:471
where the time goes:
time: 85.9 us; the launch traced here: 87.5 us
  Pallas kernels  44.7 us (52%)
  blocking collectives  20.9 us (24%)
  starting transfers between devices  17.4 us (20%)
  local copies, waits for them, and re-layouts  1.81 us (2%)
  other arithmetic  1.77 us (2%)
    ppermute x8, starting transfers between devices, shifted(): lax.ppermute(x, axis, [(i, (i + step) % count) for i in range(count)])  17.4 us
    pallas_call x1, Pallas kernels, on_device(): call(functools.partial(advance, nbrick, cap), [struct(3, nx, ny, nz), str...  12.9 us
    all_to_all x1, blocking collectives, on_device(): lax.all_to_all(answers, 'brick', split_axis=0, concat_axis=0, tiled=True)  11.3 us
    all_to_all x1, blocking collectives, on_device(): lax.all_to_all(outgoing.reshape(nbrick, 3 * chunk, width), 'brick', split...  9.58 us
    pallas_call x1, Pallas kernels, on_device(): call(functools.partial(first_deposit, nbrick, cap), [struct(4 * columns,...  8.55 us
    pallas_call x1, Pallas kernels, on_device(): call(own_contacts, [struct((nblocks + 1) * 32, width), struct((nblocks +...  8.31 us
    pallas_call x1, Pallas kernels, on_device(): call(functools.partial(last_sample, nbrick, cap), [struct(nbrick * back,...  6.75 us
    pallas_call x1, Pallas kernels, on_device(): call(functools.partial(ghost_contacts, nbrick, cap, 4 * per), [struct(3,...  5.72 us
  transfers between devices with their start and end apart: 8, of which 0 were waited for; matrix products, arithmetic and copies ran while one was open for 0% of the time, Pallas kernels for 27%

commit v1 on v0

--- a/solution.py
+++ b/solution.py
@@ -226,8 +226,8 @@
 
 
 def ghost_contacts(nbrick, cap, partner_blocks, home_list, partner_list, routes, below, above, before, after,
-                   home_side, own_sums, state, fluid,
-                   updated, outgoing, diffused,
+                   home_side, own_sums, state, cell, fluid,
+                   updated, outgoing, diffused, goals,
                    rows, columns, values, sums, homes, partners, taken,
                    home_ref, partner_ref, route_ref, flow, sems):
     nblocks, width = state.shape[1:]
@@ -267,7 +267,7 @@
         friction = total(c + 3) - speed * weights
         updated[c] = speed + (stiffness * spring + damping * friction) * inverse
 
-    chunk = rows_up(5 * cap + 1)
+    chunk, back = rows_up(5 * cap + 1), rows_up(3 * cap)
     for code in range(3 * nbrick):
         taken[code] = 0
 
@@ -275,11 +275,13 @@
         code = route_ref[b]
         spot = taken[code]
         taken[code] = spot + 1
-        row = ((code % nbrick) * 3 + code // nbrick) * chunk + spot
+        place = (code % nbrick) * 3 + code // nbrick
+        row = place * chunk + spot
+        goals[b] = place * back + spot
         outgoing[pl.ds(row, 1), :] = state[3, pl.ds(b, 1), :]
         for c in range(3):
             outgoing[pl.ds(row + (c + 1) * cap, 1), :] = updated[c, pl.ds(b, 1), :]
-        outgoing[pl.ds(row + 4 * cap, 1), :] = state[planes, pl.ds(b, 1), :]
+        outgoing[pl.ds(row + 4 * cap, 1), :] = cell[pl.ds(b, 1), :].astype(f32)
         return 0
 
     lax.fori_loop(0, nblocks, send, 0, unroll=4)
@@ -306,20 +308,26 @@
 def cell_parts(arrived, row, cap, depth):
     cell = arrived[pl.ds(row + 4 * cap, 1), :].astype(jnp.int32)
     shift = depth.bit_length() - 1
-    return cell >> shift, cell & (depth - 1)
-
-
-def level_hot(level, depth):
-    width = level.shape[1]
-    return jnp.where(iota((depth, width), 0) == level, 1.0, 0.0).astype(bf16)
+    return cell >> shift, (cell & (depth - 1)) - depth // 2
+
+
+def all_levels(depth, width):
+    return (iota((depth, width), 0) - depth // 2).astype(f32).astype(bf16)
+
+
+def level_hot(level, levels):
+    hit = levels == jnp.broadcast_to(level.astype(f32).astype(bf16), levels.shape)
+    return jnp.where(hit, jnp.ones((), bf16), jnp.zeros((), bf16))
 
 
 def deposit(count, arrived, places, cap, total):
     columns, depth = total.shape[0] // 4, total.shape[1]
     width = arrived.shape[1]
+    numbers = iota((columns, width), 0).astype(f32).astype(bf16)
+    levels = iota((width, depth), 1) - depth // 2
 
     def some(step, _):
-        loads_of, levels_of = [], []
+        high_of, low_of, level_of = [], [], []
         for k in range(GROUP):
             index = step * GROUP + k
             row = places[0][index]
@@ -327,19 +335,26 @@
             radius = arrived[pl.ds(row, 1), :]
             mass = radius * radius * radius * jnp.where(index < count, 1.0, 0.0)
             loads = [mass] + [mass * arrived[pl.ds(row + c * cap, 1), :] for c in (1, 2, 3)]
-            hit = iota((columns, width), 0) == column
+            column = jnp.broadcast_to(column.astype(f32).astype(bf16), (columns, width))
+            hit = numbers == column
             highs, lows = [], []
             for load in loads:
-                high = rounded(load)
-                highs.append(jnp.where(hit, high, 0.0).astype(bf16))
-                lows.append(jnp.where(hit, load - high, 0.0).astype(bf16))
-            hot = level_hot(level, depth)
-            loads_of += [jnp.concatenate(highs, axis=0), jnp.concatenate(lows, axis=0)]
-            levels_of += [hot, hot]
-        total[...] += lax.dot_general(
-            jnp.concatenate(loads_of, axis=1),
-            jnp.concatenate(levels_of, axis=1),
-            (((1,), (1,)), ((), ())),
+                high = load.astype(bf16)
+                low = (load - high.astype(f32)).astype(bf16)
+                for parts, part in ((highs, high), (lows, low)):
+                    part = jnp.broadcast_to(part, (columns, width))
+                    parts.append(jnp.where(hit, part, jnp.zeros((), bf16)))
+            high_of.append(jnp.concatenate(highs, axis=0))
+            low_of.append(jnp.concatenate(lows, axis=0))
+            level_of.append(level.astype(f32))
+        turned = jnp.transpose(jnp.concatenate(level_of * (8 // GROUP), axis=0)).astype(jnp.int32)
+        hots = [
+            jnp.where(levels == turned[:, k : k + 1], 1.0, 0.0).astype(bf16)
+            for k in range(GROUP)
+        ]
+        total[...] += jnp.dot(
+            jnp.concatenate(high_of + low_of, axis=1),
+            jnp.concatenate(hots + hots, axis=0),
             preferred_element_type=f32,
         )
         return 0
@@ -348,23 +363,25 @@
 
 
 def sample(count, arrived, places, cap, table, answers):
-    depth = table.shape[1]
-    columns = table.shape[0] // 6
+    depth = table.shape[1] // 2
+    columns = table.shape[0] // 3
     width = arrived.shape[1]
+    levels = all_levels(depth, width)
 
     def some(step, _):
         hots, hits = [], []
         for k in range(GROUP):
             column, level = cell_parts(arrived, places[0][step * GROUP + k], cap, depth)
-            hots.append(level_hot(level, depth))
+            hots.append(level_hot(level, levels))
             hits.append(iota((columns, width), 0) == column)
-        along = jnp.dot(table[...], jnp.concatenate(hots, axis=1), preferred_element_type=f32)
+        hot = jnp.concatenate(hots, axis=1)
+        along = jnp.dot(
+            table[...], jnp.concatenate([hot, hot], axis=0), preferred_element_type=f32
+        )
         for k in range(GROUP):
             goal = places[1][step * GROUP + k]
-            part = along[:, k * width : (k + 1) * width]
             for c in range(3):
-                value = part[c * columns : (c + 1) * columns]
-                value = value + part[(c + 3) * columns : (c + 4) * columns]
+                value = along[c * columns : (c + 1) * columns, k * width : (k + 1) * width]
                 found = jnp.sum(jnp.where(hits[k], value, 0.0), axis=0, keepdims=True)
                 answers[pl.ds(goal + c * cap, 1), :] = found
         return 0
@@ -407,10 +424,8 @@
             fresh_flow[c, x] = fresh
             high = fresh.astype(bf16)
             at = c * columns + x * ny
-            table[at : at + ny, :] = high
-            table[at + 3 * columns : at + 3 * columns + ny, :] = (
-                fresh - high.astype(f32)
-            ).astype(bf16)
+            table[at : at + ny, 0:nz] = high
+            table[at : at + ny, nz:] = (fresh - high.astype(f32)).astype(bf16)
     writing = pltpu.make_async_copy(fresh_flow, fluid_next, sems.at[1])
     writing.start()
     sample(count, arrived, (base, goal), cap, table, answers)
@@ -428,21 +443,14 @@
     sample(count, crossed, (base, goal), cap, table, answers)
 
 
-def relax(nbrick, cap, route_ref, updated, returned, velocity_next, picked, taken):
-    back = rows_up(3 * cap)
-    for code in range(3 * nbrick):
-        taken[code] = 0
-
+def relax(cap, goals, updated, returned, velocity_next, picked):
     def one(b, _):
-        code = route_ref[b]
-        spot = taken[code]
-        taken[code] = spot + 1
-        row = ((code % nbrick) * 3 + code // nbrick) * back + spot
+        row = goals[b]
         for c in range(3):
             picked[c, pl.ds(b, 1), :] = returned[pl.ds(row + c * cap, 1), :]
         return 0
 
-    lax.fori_loop(0, updated.shape[1], one, 0, unroll=4)
+    lax.fori_loop(0, updated.shape[1], one, 0, unroll=8)
     now = updated[...]
     velocity_next[...] = now + relaxation * (picked[...] - now)
 
@@ -473,9 +481,7 @@
     def ints(count):
         return pltpu.SMEM((count,), jnp.int32)
 
-    state = jnp.concatenate(
-        [positions, radii[None], velocities, cell_of.astype(f32)[None]], axis=0
-    )
+    state = jnp.concatenate([positions, radii[None], velocities], axis=0)
     ghost_rows, chunks = planes * per, 3 * (nz // width)
     up, down, right, left = call(
         pack_kernel,
@@ -506,10 +512,11 @@
         "own_contacts",
         contact_flops,
     )(tile_home, tile_partner, state)
-    updated, outgoing, diffused = call(
+    updated, outgoing, diffused, goals = call(
         functools.partial(ghost_contacts, nbrick, cap, 4 * per),
-        [struct(3, nblocks, width), struct(nbrick * 3 * chunk, width), struct(3, nx, ny, nz)],
-        [HBM] * 3 + [VMEM] * 7 + [HBM],
+        [struct(3, nblocks, width), struct(nbrick * 3 * chunk, width), struct(3, nx, ny, nz)]
+        + [struct(nblocks, dtype=jnp.int32)],
+        [HBM] * 3 + [VMEM] * 8 + [HBM],
         sides(4 * per)
         + [pltpu.VMEM(((nblocks + 1) * 16, width), f32)]
         + lists
@@ -517,8 +524,9 @@
         + [pltpu.VMEM((3, nx, ny, nz), f32), pltpu.SemaphoreType.DMA((4,))],
         "ghost_contacts",
         contact_flops // 2,
+        places=[VMEM] * 3 + [SMEM],
     )(tile_home, tile_partner, routes, below, above, before, after,
-      home_side, sums, state, fluid)
+      home_side, sums, state, cell_of, fluid)
 
     crossed = lax.all_to_all(
         outgoing.reshape(nbrick, 3 * chunk, width), "brick", split_axis=0, concat_axis=0, tiled=True
@@ -543,7 +551,7 @@
         functools.partial(advance, nbrick, cap),
         [
             struct(3, nx, ny, nz),
-            struct(6 * columns, nz, dtype=bf16),
+            struct(3 * columns, 2 * nz, dtype=bf16),
             struct(nbrick * back, width),
             struct(nbrick * back, width),
         ],
@@ -575,12 +583,12 @@
     )
     returned = lax.all_to_all(answers, "brick", split_axis=0, concat_axis=0, tiled=True)
     (velocity_next,) = call(
-        functools.partial(relax, nbrick, cap),
+        functools.partial(relax, cap),
         [struct(3, nblocks, width)],
         [SMEM] + [VMEM] * 2,
-        [pltpu.VMEM((3, nblocks, width), f32), ints(codes)],
+        [pltpu.VMEM((3, nblocks, width), f32)],
         "relax",
-    )(routes, updated, returned.reshape(nbrick * 3 * back, width))
+    )(goals, updated, returned.reshape(nbrick * 3 * back, width))
     return (jnp.transpose(velocity_next, (1, 0, 2)), fluid_next)
 
 

time: 85.9 us -> 91.8 us (1.069)
  Pallas kernels: 44.7 us -> 54.3 us
  blocking collectives: 20.9 us -> 17.5 us
    pallas_call x1, Pallas kernels: 12.9 us -> 29.6 us  [on_device(): call(functools.partial(advance, nbrick, cap), [struct(3, nx, ny, nz), str...]
    pallas_call x1, Pallas kernels: 8.55 us -> 4.82 us  [on_device(): call(functools.partial(first_deposit, nbrick, cap), [struct(4 * columns,...]
    pallas_call x1, Pallas kernels: 6.75 us -> 3.24 us  [on_device(): call(functools.partial(last_sample, nbrick, cap), [struct(nbrick * back,...]
    all_to_all x1, blocking collectives: 11.3 us -> 8.24 us  [on_device(): lax.all_to_all(answers, 'brick', split_axis=0, concat_axis=0, tiled=True)]
  transfers between devices with their start and end apart: 8 -> 8, of which waited for: 0 -> 0; matrix products, arithmetic and copies ran while one was open for 0% -> 0% of each run, Pallas kernels for 27% -> 18%
where the time goes in v1:
time: 91.8 us; the launch traced here: 92.9 us
  Pallas kernels  54.3 us (59%)
  blocking collectives  17.5 us (19%)
  starting transfers between devices  17.4 us (19%)
  local copies, waits for them, and re-layouts  1.82 us (2%)
  other arithmetic  1.01 us (1%)
    pallas_call x1, Pallas kernels, on_device(): call(functools.partial(advance, nbrick, cap), [struct(3, nx, ny, nz), str...  29.6 us
    ppermute x8, starting transfers between devices, shifted(): lax.ppermute(x, axis, [(i, (i + step) % count) for i in range(count)])  17.4 us
    all_to_all x1, blocking collectives, on_device(): lax.all_to_all(outgoing.reshape(nbrick, 3 * chunk, width), 'brick', split...  9.29 us
    pallas_call x1, Pallas kernels, on_device(): call(own_contacts, [struct((nblocks + 1) * 32, width), struct((nblocks +...  8.7 us
    all_to_all x1, blocking collectives, on_device(): lax.all_to_all(answers, 'brick', split_axis=0, concat_axis=0, tiled=True)  8.24 us
    pallas_call x1, Pallas kernels, on_device(): call(functools.partial(ghost_contacts, nbrick, cap, 4 * per), [struct(3,...  5.98 us
    pallas_call x1, Pallas kernels, on_device(): call(functools.partial(first_deposit, nbrick, cap), [struct(4 * columns,...  4.82 us
    pallas_call x1, Pallas kernels, on_device(): call(functools.partial(last_sample, nbrick, cap), [struct(nbrick * back,...  3.24 us
  transfers between devices with their start and end apart: 8, of which 0 were waited for; matrix products, arithmetic and copies ran while one was open for 0% of the time, Pallas kernels for 18%

profile of v1, /device:TPU:0, one launch (start us, length us, event | category | flops | bytes accessed | tf_op | source)
XLA Modules:
  0.0 92.9 jit_solution(796904396727956726)
XLA Ops:
  0.7 1.0 %pad_maximum_fusion.1.state = f32[7,64,128]{2,1,0:T(8,128)S(1)} fusion(f32[3,64,128]{2,1,0:T(8,128)} %bitcast.23, f32[1,64,128]{2,1,0:T(8,128)} %bitcast.26, f32[3,64,128]{2,1,0:T(8,128)} %bitcast.24), kind=kLoop, calls=%fused_computation.1 | loop fusion | flops 114688 | bytes 458752 | tf_op jit(solution)/shard_map/concatenate | solution.py:484
  1.6 0.0 copy-start
  1.7 1.1 %copy-done = f32[3,4,32,512]{3,2,1,0:T(8,128)S(1)} copy-done((f32[3,4,32,512]{3,2,1,0:T(8,128)S(1)}, f32[3,4,32,512]{3,2,1,0:T(8,128)}, u32[]{:S(2)}) %copy-start) | copy-done | bytes 786456
  2.8 0.7 copy-done.3
  3.4 0.7 pack.1
  4.1 3.0 %collective-permute-start = (f32[440,128]{1,0:T(8,128)S(1)}, f32[440,128]{1,0:T(8,128)S(1)}, u32[]{:S(2)}, u32[]{:S(2)}) collective-permute-start(f32[440,128]{1,0:T(8,128)S(1)} %get-tuple-element.16), channel_id=1, source_target_pairs={{0,4},{4,8},{8,12},{12,16},{16,20},{20,24},{24,28},{28,0},{1,5},{5... | collective-permute-start | bytes 675848 | tf_op jit(solution)/shard_map/ppermute | solution.py:479
  7.1 3.1 %collective-permute-start.1 = (f32[440,128]{1,0:T(8,128)S(1)}, f32[440,128]{1,0:T(8,128)S(1)}, u32[]{:S(2)}, u32[]{:S(2)}) collective-permute-start(f32[440,128]{1,0:T(8,128)S(1)} %get-tuple-element.17), channel_id=1, source_target_pairs={{0,28},{4,0},{8,4},{12,8},{16,12},{20,16},{24,20},{28,24},{1,29},{... | collective-permute-start | bytes 675848 | tf_op jit(solution)/shard_map/ppermute | solution.py:479
  10.2 0.0 collective-permute-start.2
  10.2 1.7 %collective-permute-start.3 = (f32[104,128]{1,0:T(8,128)S(1)}, f32[104,128]{1,0:T(8,128)S(1)}, u32[]{:S(2)}, u32[]{:S(2)}) collective-permute-start(f32[104,128]{1,0:T(8,128)S(1)} %get-tuple-element.19), channel_id=1, source_target_pairs={{0,3},{1,0},{2,1},{3,2},{4,7},{5,4},{6,5},{7,6},{8,11},{9,8},{10,9... | collective-permute-start | bytes 159752 | tf_op jit(solution)/shard_map/ppermute | solution.py:479
  12.0 8.7 %own_contacts.1 = (f32[2080,128]{1,0:T(8,128)S(1)}, f32[1040,128]{1,0:T(8,128)S(1)}) custom-call(s32[128]{0:T(128)S(1)} %copy-done.4, s32[128]{0:T(128)S(1)} %copy-done.5, f32[7,64,128]{2,1,0:T(8,128)S(1)} %pad_maximum_fusion.1.state), custom_call_target="tpu_custom_call" | custom-call | flops 419430400 | bytes 1048576 | tf_op jit(solution)/shard_map/own_contacts/pallas_call | solution.py:507
  20.7 0.0 collective-permute-done.3.after
  20.7 0.0 collective-permute-done.below
  20.8 6.0 %ghost_contacts.1 = (f32[3,64,128]{2,1,0:T(8,128)S(1)}, f32[672,128]{1,0:T(8,128)S(1)}, f32[3,4,32,512]{3,2,1,0:T(8,128)S(1)}, s32[64]{0:T(128)S(1)}) custom-call(s32[128]{0:T(128)S(1)} %copy-done.4, s32[128]{0:T(128)S(1)} %copy-done.5, s32[64]{0:T(128)S(1)} %bitcast.18, f32[440,128]{1,0:T(8,128)S(1)} %collective-permute-done.below, ...), custom_call_target="tpu_custom_call" | custom-call | flops 209715200 | bytes 1048576 | tf_op jit(solution)/shard_map/ghost_contacts/pallas_call | solution.py:515
  26.8 9.3 %all_to_all.10 = f32[4,168,128]{2,1,0:T(8,128)S(1)} all-to-all(f32[4,168,128]{2,1,0:T(8,128)S(1)} %bitcast.16), channel_id=1, replica_groups=mesh['slab'=8,'brick'=4] {'brick'}, dimensions={0} | all-to-all | bytes 688128 | tf_op jit(solution)/shard_map/all_to_all | solution.py:531
  36.1 0.1 collective-permute-start.5
  36.1 4.7 %collective-permute-start.4 = (f32[4,56,128]{2,1,0:T(8,128)S(1)}, f32[4,56,128]{2,1,0:T(8,128)S(1)}, u32[]{:S(2)}, u32[]{:S(2)}) collective-permute-start(f32[4,56,128]{2,1,0:T(8,128)S(1)} %get-tuple-element.31), channel_id=1, source_target_pairs={{0,28},{4,0},{8,4},{12,8},{16,12},{20,16},{24,20},{28,24},{1,29},{... | collective-permute-start | bytes 344072 | tf_op jit(solution)/shard_map/ppermute | solution.py:479
  40.8 4.8 %first_deposit.1.start = f32[512,512]{1,0:T(8,128)S(1)} custom-call(f32[672,128]{1,0:T(8,128)S(1)} %bitcast.14), custom_call_target="tpu_custom_call" | custom-call | flops 2863311616 | bytes 1048576 | tf_op jit(solution)/shard_map/first_deposit/pallas_call | solution.py:542
  45.7 0.0 collective-permute-done.5
  45.7 29.6 %advance.1 = (f32[3,4,32,512]{3,2,1,0:T(8,128)}, bf16[384,1024]{1,0:T(8,128)(2,1)S(1)}, f32[160,128]{1,0:T(8,128)S(1)}, f32[160,128]{1,0:T(8,128)S(1)}) custom-call(f32[224,128]{1,0:T(8,128)S(1)} %bitcast.20, f32[224,128]{1,0:T(8,128)S(1)} %bitcast.19, f32[512,512]{1,0:T(8,128)S(1)} %first_deposit.1.start, f32[3,4,32,512]{3,2,1,0:T(8,128)S(1)} %copy-done.1, ...), custom_call_target="tpu_custom_call" | custom-call | flops 8589934592 | bytes 1048576 | tf_op jit(solution)/shard_map/advance/pallas_call | solution.py:550
  75.3 0.1 collective-permute-start.6
  75.4 4.7 %collective-permute-start.7 = (f32[4,40,128]{2,1,0:T(8,128)S(1)}, f32[4,40,128]{2,1,0:T(8,128)S(1)}, u32[]{:S(2)}, u32[]{:S(2)}) collective-permute-start(f32[4,40,128]{2,1,0:T(8,128)S(1)} %bitcast.21), channel_id=1, source_target_pairs={{0,28},{4,0},{8,4},{12,8},{16,12},{20,16},{24,20},{28,24},{1,29},{... | collective-permute-start | bytes 245768 | tf_op jit(solution)/shard_map/ppermute | solution.py:479
  80.1 3.2 %last_sample.1 = f32[160,128]{1,0:T(8,128)S(1)} custom-call(f32[672,128]{1,0:T(8,128)S(1)} %bitcast.15, bf16[384,1024]{1,0:T(8,128)(2,1)S(1)} %get-tuple-element.27.table), custom_call_target="tpu_custom_call" | custom-call | flops 2147483648 | bytes 1048576 | tf_op jit(solution)/shard_map/last_sample/pallas_call | solution.py:573
  83.4 8.2 %all_to_all.11 = f32[4,120,128]{2,1,0:T(8,128)S(1)} all-to-all(f32[4,120,128]{2,1,0:T(8,128)S(1)} %pad_maximum_fusion), channel_id=1, replica_groups=mesh['slab'=8,'brick'=4] {'brick'}, dimensions={0} | all-to-all | bytes 491520 | tf_op jit(solution)/shard_map/all_to_all | solution.py:584
  91.6 1.3 %relax.1 = f32[3,64,128]{2,1,0:T(8,128)} custom-call(s32[64]{0:T(128)S(1)} %get-tuple-element.22.goals, f32[3,64,128]{2,1,0:T(8,128)S(1)} %get-tuple-element.23.updated, f32[480,128]{1,0:T(8,128)S(1)} %bitcast.13), custom_call_target="tpu_custom_call" | custom-call | bytes 1048576 | tf_op jit(solution)/shard_map/relax/pallas_call | solution.py:585
  (18 shorter events, 0.1 us)
Async XLA Ops:
  0.6 11.3 %copy-start.5 = (s32[128]{0:T(128)S(1)}, s32[128]{0:T(128)}, u32[]{:S(2)}) copy-start(s32[128]{0:T(128)} %partner_list.3) | copy-start | bytes 1540
  0.6 11.3 %copy-start.4 = (s32[128]{0:T(128)S(1)}, s32[128]{0:T(128)}, u32[]{:S(2)}) copy-start(s32[128]{0:T(128)} %home_list.3) | copy-start | bytes 1540
  1.6 1.1 %copy-start = (f32[3,4,32,512]{3,2,1,0:T(8,128)S(1)}, f32[3,4,32,512]{3,2,1,0:T(8,128)}, u32[]{:S(2)}) copy-start(f32[3,4,32,512]{3,2,1,0:T(8,128)} %fluid.5) | copy-start | bytes 2359300
  2.8 0.7 copy-start.3
  3.4 17.3 %copy-start.1 = (f32[3,4,32,512]{3,2,1,0:T(8,128)S(1)}, f32[3,4,32,512]{3,2,1,0:T(8,128)}, u32[]{:S(2)}) copy-start(f32[3,4,32,512]{3,2,1,0:T(8,128)} %fluid.5) | copy-start | bytes 2359300
  3.4 17.3 %copy-start.2 = (s32[64,128]{1,0:T(8,128)S(1)}, s32[64,128]{1,0:T(8,128)}, u32[]{:S(2)}) copy-start(s32[64,128]{1,0:T(8,128)} %cell.1) | copy-start | bytes 98308
  3.4 17.3 %copy-start.6 = (s32[64,1]{0,1:T(1,128)S(1)}, s32[64,1]{0,1:T(1,128)}, u32[]{:S(2)}) copy-start(s32[64,1]{0,1:T(1,128)} %param.13) | copy-start | bytes 772
  4.1 16.6 %collective-permute-start = (f32[440,128]{1,0:T(8,128)S(1)}, f32[440,128]{1,0:T(8,128)S(1)}, u32[]{:S(2)}, u32[]{:S(2)}) collective-permute-start(f32[440,128]{1,0:T(8,128)S(1)} %get-tuple-element.16), channel_id=1, source_target_pairs={{0,4},{4,8},{8,12},{12,16},{16,20},{20,24},{24,28},{28,0},{1,5},{5... | collective-permute-start | bytes 675848 | tf_op jit(solution)/shard_map/ppermute | solution.py:479
  7.1 13.6 %collective-permute-start.1 = (f32[440,128]{1,0:T(8,128)S(1)}, f32[440,128]{1,0:T(8,128)S(1)}, u32[]{:S(2)}, u32[]{:S(2)}) collective-permute-start(f32[440,128]{1,0:T(8,128)S(1)} %get-tuple-element.17), channel_id=1, source_target_pairs={{0,28},{4,0},{8,4},{12,8},{16,12},{20,16},{24,20},{28,24},{1,29},{... | collective-permute-start | bytes 675848 | tf_op jit(solution)/shard_map/ppermute | solution.py:479
  10.2 10.5 %collective-permute-start.2 = (f32[104,128]{1,0:T(8,128)S(1)}, f32[104,128]{1,0:T(8,128)S(1)}, u32[]{:S(2)}, u32[]{:S(2)}) collective-permute-start(f32[104,128]{1,0:T(8,128)S(1)} %get-tuple-element.18), channel_id=1, source_target_pairs={{0,1},{1,2},{2,3},{3,0},{4,5},{5,6},{6,7},{7,4},{8,9},{9,10},{10,1... | collective-permute-start | bytes 159752 | tf_op jit(solution)/shard_map/ppermute | solution.py:479
  10.2 10.5 %collective-permute-start.3 = (f32[104,128]{1,0:T(8,128)S(1)}, f32[104,128]{1,0:T(8,128)S(1)}, u32[]{:S(2)}, u32[]{:S(2)}) collective-permute-start(f32[104,128]{1,0:T(8,128)S(1)} %get-tuple-element.19), channel_id=1, source_target_pairs={{0,3},{1,0},{2,1},{3,2},{4,7},{5,4},{6,5},{7,6},{8,11},{9,8},{10,9... | collective-permute-start | bytes 159752 | tf_op jit(solution)/shard_map/ppermute | solution.py:479
  36.1 9.6 %collective-permute-start.5 = (f32[4,56,128]{2,1,0:T(8,128)S(1)}, f32[4,56,128]{2,1,0:T(8,128)S(1)}, u32[]{:S(2)}, u32[]{:S(2)}) collective-permute-start(f32[4,56,128]{2,1,0:T(8,128)S(1)} %get-tuple-element.30), channel_id=1, source_target_pairs={{0,4},{4,8},{8,12},{12,16},{16,20},{20,24},{24,28},{28,0},{1,5},{5... | collective-permute-start | bytes 344072 | tf_op jit(solution)/shard_map/ppermute | solution.py:479
  36.1 9.6 %collective-permute-start.4 = (f32[4,56,128]{2,1,0:T(8,128)S(1)}, f32[4,56,128]{2,1,0:T(8,128)S(1)}, u32[]{:S(2)}, u32[]{:S(2)}) collective-permute-start(f32[4,56,128]{2,1,0:T(8,128)S(1)} %get-tuple-element.31), channel_id=1, source_target_pairs={{0,28},{4,0},{8,4},{12,8},{16,12},{20,16},{24,20},{28,24},{1,29},{... | collective-permute-start | bytes 344072 | tf_op jit(solution)/shard_map/ppermute | solution.py:479
  75.3 8.0 %collective-permute-start.6 = (f32[4,40,128]{2,1,0:T(8,128)S(1)}, f32[4,40,128]{2,1,0:T(8,128)S(1)}, u32[]{:S(2)}, u32[]{:S(2)}) collective-permute-start(f32[4,40,128]{2,1,0:T(8,128)S(1)} %bitcast.22), channel_id=1, source_target_pairs={{0,4},{4,8},{8,12},{12,16},{16,20},{20,24},{24,28},{28,0},{1,5},{5... | collective-permute-start | bytes 245768 | tf_op jit(solution)/shard_map/ppermute | solution.py:479
  75.4 8.0 %collective-permute-start.7 = (f32[4,40,128]{2,1,0:T(8,128)S(1)}, f32[4,40,128]{2,1,0:T(8,128)S(1)}, u32[]{:S(2)}, u32[]{:S(2)}) collective-permute-start(f32[4,40,128]{2,1,0:T(8,128)S(1)} %bitcast.21), channel_id=1, source_target_pairs={{0,28},{4,0},{8,4},{12,8},{16,12},{20,16},{24,20},{28,24},{1,29},{... | collective-permute-start | bytes 245768 | tf_op jit(solution)/shard_map/ppermute | solution.py:479

commit v2 on v1

--- a/solution.py
+++ b/solution.py
@@ -18,6 +18,7 @@
 bf16 = jnp.bfloat16
 VMEM = pl.BlockSpec(memory_space=pltpu.VMEM)
 SMEM = pl.BlockSpec(memory_space=pltpu.SMEM)
+ANY = pl.BlockSpec(memory_space=pl.ANY)
 HBM = pl.BlockSpec(memory_space=pltpu.HBM)
 UNROLL = 8
 GROUP = 4
@@ -183,18 +184,103 @@
     lax.fori_loop(0, (count + UNROLL - 1) // UNROLL, some, 0)
 
 
-def own_contacts(home_list, partner_list, state, home_side, sums,
-                 rows, columns, values, homes, partners, home_ref, partner_ref, sems):
+def dot(left, right):
+    return jnp.dot(left.astype(bf16), right.astype(bf16), preferred_element_type=f32)
+
+
+def plan_sort(codes, cell, route, columns, depth, spots, plan, bounds):
+    nblocks, width = cell.shape
+    shift = depth.bit_length() - 1
+    number = cell[...]
+    right = (number >> shift) >= columns // 2
+    deep = (number & (depth - 1)) >= depth // 2
+    kind = jnp.where(right, 2, 0) + jnp.where(deep, 1, 0)
+    members = [jnp.where(kind == j, 1.0, 0.0) for j in range(4)]
+    before = jnp.where(iota((width, width), 0) < iota((width, width), 1), 1.0, 0.0)
+    stacked = jnp.concatenate(members, axis=0)
+    ranks = dot(stacked, before)
+    lengths = dot(stacked, jnp.ones((width, width), f32))
+    ranks = [ranks[j * nblocks : (j + 1) * nblocks] for j in range(4)]
+    lengths = [lengths[j * nblocks : (j + 1) * nblocks] for j in range(4)]
+
+    across = jnp.broadcast_to(route[...].astype(f32), (nblocks, nblocks))
+    same = across == jnp.transpose(across)
+    earlier = iota((nblocks, nblocks), 1) < iota((nblocks, nblocks), 0)
+    side_by_side = jnp.concatenate(lengths, axis=1)
+    ahead = dot(jnp.where(same & earlier, 1.0, 0.0), side_by_side)
+    whole = dot(jnp.where(same, 1.0, 0.0), side_by_side)
+    rows = bounds.shape[0]
+    of_code = jnp.broadcast_to(route[...], (rows, nblocks)) == iota((rows, nblocks), 0)
+    totals = dot(jnp.where(of_code, 1.0, 0.0), side_by_side)
+
+    lane = iota((nblocks, width), 1)
+    bound_lane = iota((rows, width), 1)
+    spot = jnp.zeros((nblocks, width), f32)
+    first, chunk_first = jnp.zeros((nblocks, width), f32), jnp.zeros((nblocks, width), f32)
+    bound, line = jnp.zeros((rows, width), f32), jnp.zeros((rows, width), f32)
+    table = jnp.zeros((nblocks, width), f32)
+    for j in range(4):
+        at = slice(j * width, (j + 1) * width)
+        spot = spot + members[j] * (first + ranks[j])
+        table = jnp.where(lane == j, chunk_first + ahead[:, at], table)
+        table = jnp.where(lane == 4 + j, first, table)
+        table = jnp.where(lane == 8 + j, lengths[j], table)
+        first = first + lengths[j]
+        chunk_first = chunk_first + whole[:, at]
+        bound = bound + totals[:, at]
+        line = jnp.where(bound_lane == j, bound, line)
+    spots[...] = spot
+    plan[...] = table.astype(jnp.int32)
+    bounds[...] = line
+
+
+def place_of(plan, b, j, width):
+    at = plan[b, j]
+    return at // width, at % width, plan[b, 4 + j], plan[b, 8 + j]
+
+
+def block_order(spots, b):
+    width = spots.shape[1]
+    row = jnp.broadcast_to(spots[pl.ds(b, 1), :], (width, width))
+    return jnp.where(iota((width, width), 0).astype(f32) == row, 1.0, 0.0).astype(bf16)
+
+
+def sort_blocks(route_ref, plan, spots, data, tiles, cap):
+    nblocks, width = spots.shape
+    lane = iota((8, width), 1)
+
+    def one(b, _):
+        rows = data[pl.ds(pl.multiple_of(b * 16, 16), 16), :].astype(bf16)
+        both = lax.dot_general(
+            rows, block_order(spots, b), (((1,), (1,)), ((), ())), preferred_element_type=f32
+        )
+        block = both[0:8] + both[8:16]
+        chunk = route_ref[b] * (cap + 2)
+        for j in range(4):
+            tile, at, first, length = place_of(plan, b, j, width)
+            moved = pltpu.roll(block, (at - first + width) % width, 1)
+            now, later = chunk + tile, chunk + tile + 1
+            tiles[now] = jnp.where((lane >= at) & (lane < at + length), moved, tiles[now])
+            tiles[later] = jnp.where(lane < at + length - width, moved, tiles[later])
+        return 0
+
+    lax.fori_loop(0, nblocks, one, 0, unroll=4)
+
+
+def own_contacts(codes, columns, depth, home_list, partner_list, state, cell, route,
+                 home_side, sums, spots, plan, bounds,
+                 rows, partner_side, values, homes, partners, home_ref, partner_ref, sems):
     nblocks, width = state.shape[1:]
     copies = copy_all([(home_list, home_ref), (partner_list, partner_ref)], sems)
+    plan_sort(codes, cell, route, columns, depth, spots, plan, bounds)
     place = [state[c] for c in range(4)]
     put_rows(home_side, 32, home_rows(place))
-    prepare_partners(place, [state[c] for c in (4, 5, 6)], rows, columns, values)
+    prepare_partners(place, [state[c] for c in (4, 5, 6)], rows, partner_side, values)
     home_side[nblocks * 32 :, :] = jnp.zeros((32, width), f32)
     sums[...] = jnp.zeros(sums.shape, f32)
     wait_all(copies)
     count = list_tiles(home_ref, partner_ref, homes, partners, 0, nblocks, nblocks)
-    add_tiles(count, homes, partners, home_side, columns, values, sums)
+    add_tiles(count, homes, partners, home_side, partner_side, values, sums)
 
 
 def diffuse(fluid, below, above, before, after, skip, diffused):
@@ -225,11 +311,11 @@
             diffused[c, x] = here + viscosity * (near - 6.0 * here)
 
 
-def ghost_contacts(nbrick, cap, partner_blocks, home_list, partner_list, routes, below, above, before, after,
-                   home_side, own_sums, state, cell, fluid,
-                   updated, outgoing, diffused, goals,
-                   rows, columns, values, sums, homes, partners, taken,
-                   home_ref, partner_ref, route_ref, flow, sems):
+def ghost_contacts(nbrick, cap, partner_blocks, home_list, partner_list, routes, plan, below,
+                   above, before, after, home_side, own_sums, state, cell, spots, bounds, fluid,
+                   updated, outgoing, diffused,
+                   rows, columns, values, sums, data, tiles, homes, partners,
+                   home_ref, partner_ref, route_ref, plan_ref, flow, sems):
     nblocks, width = state.shape[1:]
     per = partner_blocks // 4
     copies = copy_all(
@@ -237,6 +323,7 @@
             (home_list, home_ref),
             (partner_list, partner_ref),
             (routes, route_ref),
+            (plan, plan_ref),
             (fluid, flow),
         ],
         sems,
@@ -261,54 +348,70 @@
     weights = total(6)
     radius = state[3]
     inverse = 1.0 / (radius * radius * radius)
+    fresh = []
     for c in range(3):
         speed = state[c + 4]
         spring = state[c] * weights - total(c)
         friction = total(c + 3) - speed * weights
-        updated[c] = speed + (stiffness * spring + damping * friction) * inverse
-
-    chunk, back = rows_up(5 * cap + 1), rows_up(3 * cap)
+        fresh.append(speed + (stiffness * spring + damping * friction) * inverse)
+        updated[c] = fresh[c]
+
+    number = cell[...]
+    zeros = jnp.zeros_like(radius)
+    highs = [rounded(plane) for plane in [radius] + fresh]
+    lows = [plane - high for plane, high in zip([radius] + fresh, highs)]
+    highs.append(((number >> 8) * 256).astype(f32))
+    lows.append((number & 255).astype(f32))
+    put_rows(data, 16, highs + [zeros] * 3 + lows + [zeros] * 3)
+    sort_blocks(route_ref, plan_ref, spots, data, tiles, cap)
+
+    chunk = rows_up(5 * cap + 1)
+    flat = tiles.reshape(tiles.shape[0] * 8, width)
     for code in range(3 * nbrick):
-        taken[code] = 0
-
-    def send(b, _):
-        code = route_ref[b]
-        spot = taken[code]
-        taken[code] = spot + 1
-        place = (code % nbrick) * 3 + code // nbrick
-        row = place * chunk + spot
-        goals[b] = place * back + spot
-        outgoing[pl.ds(row, 1), :] = state[3, pl.ds(b, 1), :]
-        for c in range(3):
-            outgoing[pl.ds(row + (c + 1) * cap, 1), :] = updated[c, pl.ds(b, 1), :]
-        outgoing[pl.ds(row + 4 * cap, 1), :] = cell[pl.ds(b, 1), :].astype(f32)
-        return 0
-
-    lax.fori_loop(0, nblocks, send, 0, unroll=4)
-    for code in range(3 * nbrick):
-        row = ((code % nbrick) * 3 + code // nbrick) * chunk + 5 * cap
-        outgoing[row : row + 1, :] = jnp.full((1, width), taken[code], jnp.int32).astype(f32)
-
-
-def list_blocks(arrived, starts, ends, cap, places):
+        row = ((code % nbrick) * 3 + code // nbrick) * chunk
+        for c in range(5):
+            outgoing[row + c * cap : row + (c + 1) * cap, :] = flat[
+                pl.ds(code * (cap + 2) * 8 + c, cap, stride=8), :
+            ]
+        outgoing[row + 5 * cap : row + 5 * cap + 1, :] = bounds[code : code + 1, :]
+
+
+def list_stride(segments, cap):
+    return (segments + 1) * cap + GROUP
+
+
+def list_arrived(arrived, starts, ends, cap, places, counts):
     base, goal = places
-    count = 0
+    width = arrived.shape[1]
+    stride = list_stride(len(starts), cap)
+    lane = iota((1, width), 1)
+    filled = [jnp.int32(0)] * 4
     for start, end in zip(starts, ends):
-        here = jnp.max(arrived[start + 5 * cap : start + 5 * cap + 1, :]).astype(jnp.int32)
-        for spot in range(cap):
-            base[count] = start + spot
-            goal[count] = end + spot
-            count = count + jnp.where(spot < here, 1, 0)
-    for pad in range(GROUP):
-        base[count + pad] = base[jnp.maximum(count - 1, 0)]
-        goal[count + pad] = goal[jnp.maximum(count - 1, 0)]
-    return count
-
-
-def cell_parts(arrived, row, cap, depth):
+        row = arrived[start + 5 * cap : start + 5 * cap + 1, :]
+        edge = jnp.int32(0)
+        for j in range(4):
+            next_edge = jnp.sum(jnp.where(lane == j, row, 0.0)).astype(jnp.int32)
+            first = edge // width
+            last = jnp.where(next_edge > edge, (next_edge + width - 1) // width, first)
+            for i in range(cap):
+                base[j * stride + filled[j] + i] = start + first + i
+                goal[j * stride + filled[j] + i] = end + first + i
+            filled[j] = filled[j] + last - first
+            edge = next_edge
+    for j in range(4):
+        counts[j] = filled[j]
+        last = j * stride + jnp.maximum(filled[j] - 1, 0)
+        for pad in range(GROUP):
+            base[j * stride + filled[j] + pad] = base[last]
+            goal[j * stride + filled[j] + pad] = goal[last]
+
+
+def cell_parts(arrived, row, cap, columns, depth, bucket):
     cell = arrived[pl.ds(row + 4 * cap, 1), :].astype(jnp.int32)
-    shift = depth.bit_length() - 1
-    return cell >> shift, (cell & (depth - 1)) - depth // 2
+    shift = (2 * depth).bit_length() - 1
+    column = (cell >> shift) - (bucket // 2) * columns
+    level = (cell & (2 * depth - 1)) - (bucket % 2) * depth - depth // 2
+    return column.astype(f32), level.astype(f32)
 
 
 def all_levels(depth, width):
@@ -316,89 +419,108 @@
 
 
 def level_hot(level, levels):
-    hit = levels == jnp.broadcast_to(level.astype(f32).astype(bf16), levels.shape)
+    hit = levels == jnp.broadcast_to(level.astype(bf16), levels.shape)
     return jnp.where(hit, jnp.ones((), bf16), jnp.zeros((), bf16))
 
 
-def deposit(count, arrived, places, cap, total):
-    columns, depth = total.shape[0] // 4, total.shape[1]
+def deposit(segments, counts, arrived, base, cap, total):
+    columns, depth = total.shape[0] // 16, total.shape[1]
     width = arrived.shape[1]
+    stride = list_stride(segments, cap)
     numbers = iota((columns, width), 0).astype(f32).astype(bf16)
-    levels = iota((width, depth), 1) - depth // 2
-
-    def some(step, _):
-        high_of, low_of, level_of = [], [], []
-        for k in range(GROUP):
-            index = step * GROUP + k
-            row = places[0][index]
-            column, level = cell_parts(arrived, row, cap, depth)
-            radius = arrived[pl.ds(row, 1), :]
-            mass = radius * radius * radius * jnp.where(index < count, 1.0, 0.0)
-            loads = [mass] + [mass * arrived[pl.ds(row + c * cap, 1), :] for c in (1, 2, 3)]
-            column = jnp.broadcast_to(column.astype(f32).astype(bf16), (columns, width))
-            hit = numbers == column
-            highs, lows = [], []
-            for load in loads:
-                high = load.astype(bf16)
-                low = (load - high.astype(f32)).astype(bf16)
-                for parts, part in ((highs, high), (lows, low)):
-                    part = jnp.broadcast_to(part, (columns, width))
-                    parts.append(jnp.where(hit, part, jnp.zeros((), bf16)))
-            high_of.append(jnp.concatenate(highs, axis=0))
-            low_of.append(jnp.concatenate(lows, axis=0))
-            level_of.append(level.astype(f32))
-        turned = jnp.transpose(jnp.concatenate(level_of * (8 // GROUP), axis=0)).astype(jnp.int32)
-        hots = [
-            jnp.where(levels == turned[:, k : k + 1], 1.0, 0.0).astype(bf16)
-            for k in range(GROUP)
-        ]
-        total[...] += jnp.dot(
-            jnp.concatenate(high_of + low_of, axis=1),
-            jnp.concatenate(hots + hots, axis=0),
-            preferred_element_type=f32,
-        )
+    levels = all_levels(depth, width)
+
+    def one(bucket, _):
+        count = counts[bucket]
+
+        def some(step, _):
+            high_of, low_of, level_of = [], [], []
+            for k in range(GROUP):
+                index = step * GROUP + k
+                row = base[bucket * stride + index]
+                column, level = cell_parts(arrived, row, cap, columns, depth, bucket)
+                radius = arrived[pl.ds(row, 1), :]
+                mass = radius * radius * radius * jnp.where(index < count, 1.0, 0.0)
+                loads = [mass] + [mass * arrived[pl.ds(row + c * cap, 1), :] for c in (1, 2, 3)]
+                hit = numbers == jnp.broadcast_to(column.astype(bf16), (columns, width))
+                highs, lows = [], []
+                for load in loads:
+                    high = load.astype(bf16)
+                    low = (load - high.astype(f32)).astype(bf16)
+                    for parts, part in ((highs, high), (lows, low)):
+                        part = jnp.broadcast_to(part, (columns, width))
+                        parts.append(jnp.where(hit, part, jnp.zeros((), bf16)))
+                high_of.append(jnp.concatenate(highs, axis=0))
+                low_of.append(jnp.concatenate(lows, axis=0))
+                level_of.append(level_hot(level, levels))
+            both = lax.dot_general(
+                jnp.concatenate(
+                    [jnp.concatenate(high_of, axis=1), jnp.concatenate(low_of, axis=1)], axis=0
+                ),
+                jnp.concatenate(level_of, axis=1),
+                (((1,), (1,)), ((), ())),
+                preferred_element_type=f32,
+            )
+            at = pl.ds(pl.multiple_of(bucket * 4 * columns, 4 * columns), 4 * columns)
+            total[at, :] += both[0 : 4 * columns] + both[4 * columns :]
+            return 0
+
+        lax.fori_loop(0, (count + GROUP - 1) // GROUP, some, 0)
         return 0
 
-    lax.fori_loop(0, (count + GROUP - 1) // GROUP, some, 0)
-
-
-def sample(count, arrived, places, cap, table, answers):
-    depth = table.shape[1] // 2
-    columns = table.shape[0] // 3
+    lax.fori_loop(0, 4, one, 0)
+
+
+def sample(segments, counts, arrived, places, cap, table, answers):
+    columns, depth = table.shape[0] // 24, table.shape[1]
     width = arrived.shape[1]
+    stride = list_stride(segments, cap)
     levels = all_levels(depth, width)
-
-    def some(step, _):
-        hots, hits = [], []
-        for k in range(GROUP):
-            column, level = cell_parts(arrived, places[0][step * GROUP + k], cap, depth)
-            hots.append(level_hot(level, levels))
-            hits.append(iota((columns, width), 0) == column)
-        hot = jnp.concatenate(hots, axis=1)
-        along = jnp.dot(
-            table[...], jnp.concatenate([hot, hot], axis=0), preferred_element_type=f32
-        )
-        for k in range(GROUP):
-            goal = places[1][step * GROUP + k]
-            for c in range(3):
-                value = along[c * columns : (c + 1) * columns, k * width : (k + 1) * width]
-                found = jnp.sum(jnp.where(hits[k], value, 0.0), axis=0, keepdims=True)
-                answers[pl.ds(goal + c * cap, 1), :] = found
+    numbers = iota((columns, width), 0).astype(f32)
+    answers[...] = jnp.zeros(answers.shape, f32)
+
+    def one(bucket, _):
+        count = counts[bucket]
+
+        def some(step, _):
+            hots, hits = [], []
+            for k in range(GROUP):
+                row = places[0][bucket * stride + step * GROUP + k]
+                column, level = cell_parts(arrived, row, cap, columns, depth, bucket)
+                hots.append(level_hot(level, levels))
+                hits.append(numbers == column)
+            at = pl.ds(pl.multiple_of(bucket * 6 * columns, 6 * columns), 6 * columns)
+            along = jnp.dot(
+                table[at, :], jnp.concatenate(hots, axis=1), preferred_element_type=f32
+            )
+            for k in range(GROUP):
+                index = step * GROUP + k
+                goal = places[1][bucket * stride + index]
+                real = jnp.where(index < count, 1.0, 0.0)
+                part = along[:, k * width : (k + 1) * width]
+                for c in range(3):
+                    value = part[c * columns : (c + 1) * columns]
+                    value = value + part[(c + 3) * columns : (c + 4) * columns]
+                    found = jnp.sum(jnp.where(hits[k], value, 0.0), axis=0, keepdims=True)
+                    answers[pl.ds(goal + c * cap, 1), :] += found * real
+            return 0
+
+        lax.fori_loop(0, (count + GROUP - 1) // GROUP, some, 0)
         return 0
 
-    lax.fori_loop(0, (count + GROUP - 1) // GROUP, some, 0)
-
-
-def first_deposit(nbrick, cap, crossed, total, base, goal):
+    lax.fori_loop(0, 4, one, 0)
+
+
+def first_deposit(nbrick, cap, crossed, total, base, goal, counts):
     chunk = rows_up(5 * cap + 1)
     total[...] = jnp.zeros(total.shape, f32)
     starts = [(3 * b + 1) * chunk for b in range(nbrick)]
-    count = list_blocks(crossed, starts, starts, cap, (base, goal))
-    deposit(count, crossed, (base, goal), cap, total)
+    list_arrived(crossed, starts, starts, cap, (base, goal), counts)
+    deposit(nbrick, counts, crossed, base, cap, total)
 
 
 def advance(nbrick, cap, above, below, start, fluid, diffused, fluid_next, table, answers_up,
-            answers_down, arrived, answers, total, flow, fresh_flow, base, goal, sems):
+            answers_down, arrived, answers, total, flow, fresh_flow, base, goal, counts, sems):
     reading = pltpu.make_async_copy(fluid, flow, sems.at[0])
     reading.start()
     chunk = rows_up(5 * cap + 1)
@@ -409,48 +531,84 @@
     starts = [i * chunk for i in range(2 * nbrick)]
     ends = [i * back for i in range(2 * nbrick)]
     total[...] = start[...]
-    count = list_blocks(arrived, starts, ends, cap, (base, goal))
-    deposit(count, arrived, (base, goal), cap, total)
+    list_arrived(arrived, starts, ends, cap, (base, goal), counts)
+    deposit(2 * nbrick, counts, arrived, base, cap, total)
     reading.wait()
 
     nx, ny, nz = flow.shape[1:]
-    columns = nx * ny
+    columns, depth = nx * ny // 2, nz // 2
     for x in range(nx):
-        volume = total[x * ny : (x + 1) * ny, :]
+        buckets = [2 * (x * ny // columns) + deep for deep in range(2)]
+        at = x * ny % columns
+
+        def load(c):
+            spots = [4 * columns * bucket + c * columns + at for bucket in buckets]
+            return jnp.concatenate([total[spot : spot + ny, :] for spot in spots], axis=1)
+
+        volume = load(0)
         for c in range(3):
-            at = (c + 1) * columns + x * ny
-            moved = total[at : at + ny, :] - volume * flow[c, x]
+            moved = load(c + 1) - volume * flow[c, x]
             fresh = diffused[c, x] + coupling * moved
             fresh_flow[c, x] = fresh
             high = fresh.astype(bf16)
-            at = c * columns + x * ny
-            table[at : at + ny, 0:nz] = high
-            table[at : at + ny, nz:] = (fresh - high.astype(f32)).astype(bf16)
+            low = (fresh - high.astype(f32)).astype(bf16)
+            for deep, bucket in enumerate(buckets):
+                spot = 6 * columns * bucket + c * columns + at
+                half = slice(deep * depth, (deep + 1) * depth)
+                table[spot : spot + ny, :] = high[:, half]
+                table[spot + 3 * columns : spot + 3 * columns + ny, :] = low[:, half]
     writing = pltpu.make_async_copy(fresh_flow, fluid_next, sems.at[1])
     writing.start()
-    sample(count, arrived, (base, goal), cap, table, answers)
+    sample(2 * nbrick, counts, arrived, (base, goal), cap, table, answers)
     answers_up[...] = answers[0 : nbrick * back, :]
     answers_down[...] = answers[nbrick * back :, :]
     writing.wait()
 
 
-def last_sample(nbrick, cap, crossed, table, answers, base, goal):
+def last_sample(nbrick, cap, crossed, table, answers, base, goal, counts):
     chunk = rows_up(5 * cap + 1)
     back = rows_up(3 * cap)
     starts = [(3 * b + 1) * chunk for b in range(nbrick)]
     ends = [b * back for b in range(nbrick)]
-    count = list_blocks(crossed, starts, ends, cap, (base, goal))
-    sample(count, crossed, (base, goal), cap, table, answers)
-
-
-def relax(cap, goals, updated, returned, velocity_next, picked):
+    list_arrived(crossed, starts, ends, cap, (base, goal), counts)
+    sample(nbrick, counts, crossed, (base, goal), cap, table, answers)
+
+
+def relax(nbrick, cap, route_ref, plan, updated, returned, spots, velocity_next, picked, tiles,
+          plan_ref, sems):
+    copies = copy_all([(plan, plan_ref)], sems)
+    nblocks, width = spots.shape
+    back = rows_up(3 * cap)
+    flat = tiles.reshape(tiles.shape[0] * 8, width)
+    for code in range(3 * nbrick):
+        row = ((code % nbrick) * 3 + code // nbrick) * back
+        for c in range(3):
+            flat[pl.ds(code * (cap + 2) * 8 + c, cap, stride=8), :] = returned[
+                row + c * cap : row + (c + 1) * cap, :
+            ]
+    lane = iota((8, width), 1)
+    wait_all(copies)
+
     def one(b, _):
-        row = goals[b]
+        chunk = route_ref[b] * (cap + 2)
+        block = jnp.zeros((8, width), f32)
+        for j in range(4):
+            tile, at, first, length = place_of(plan_ref, b, j, width)
+            run = jnp.where(lane >= at, tiles[chunk + tile], tiles[chunk + tile + 1])
+            run = pltpu.roll(run, (first - at + width) % width, 1)
+            block = jnp.where((lane >= first) & (lane < first + length), run, block)
+        high = rounded(block)
+        both = jnp.dot(
+            jnp.concatenate([high, block - high], axis=0).astype(bf16),
+            block_order(spots, b),
+            preferred_element_type=f32,
+        )
+        block = both[0:8] + both[8:16]
         for c in range(3):
-            picked[c, pl.ds(b, 1), :] = returned[pl.ds(row + c * cap, 1), :]
+            picked[c, pl.ds(b, 1), :] = block[c : c + 1]
         return 0
 
-    lax.fori_loop(0, updated.shape[1], one, 0, unroll=8)
+    lax.fori_loop(0, nblocks, one, 0, unroll=4)
     now = updated[...]
     velocity_next[...] = now + relaxation * (picked[...] - now)
 
@@ -504,29 +662,36 @@
 
     lists = [ints(tiles + UNROLL)] * 2
     contact_flops = tiles * width * width * 200
-    home_side, sums = call(
-        own_contacts,
-        [struct((nblocks + 1) * 32, width), struct((nblocks + 1) * 16, width)],
-        [HBM] * 2 + [VMEM],
+    chunk_tiles = pltpu.VMEM((codes * (cap + 2), 8, width), f32)
+    plan_copy = pltpu.SMEM((nblocks, width), jnp.int32)
+    home_side, sums, spots, plan, bounds = call(
+        functools.partial(own_contacts, codes, columns, nz),
+        [
+            struct((nblocks + 1) * 32, width),
+            struct((nblocks + 1) * 16, width),
+            struct(nblocks, width),
+            struct(nblocks, width, dtype=jnp.int32),
+            struct(rows_up(codes), width),
+        ],
+        [HBM] * 2 + [VMEM] * 3,
         sides(nblocks) + lists + [ints(tiles)] * 2 + [pltpu.SemaphoreType.DMA((2,))],
         "own_contacts",
         contact_flops,
-    )(tile_home, tile_partner, state)
-    updated, outgoing, diffused, goals = call(
+    )(tile_home, tile_partner, state, cell_of, routes.reshape(1, nblocks))
+    updated, outgoing, diffused = call(
         functools.partial(ghost_contacts, nbrick, cap, 4 * per),
-        [struct(3, nblocks, width), struct(nbrick * 3 * chunk, width), struct(3, nx, ny, nz)]
-        + [struct(nblocks, dtype=jnp.int32)],
-        [HBM] * 3 + [VMEM] * 8 + [HBM],
+        [struct(3, nblocks, width), struct(nbrick * 3 * chunk, width), struct(3, nx, ny, nz)],
+        [HBM] * 3 + [ANY] + [VMEM] * 10 + [HBM],
         sides(4 * per)
         + [pltpu.VMEM(((nblocks + 1) * 16, width), f32)]
+        + [pltpu.VMEM((nblocks * 16, width), f32), chunk_tiles]
         + lists
-        + [ints(codes), ints(tiles), ints(tiles), ints(nblocks)]
-        + [pltpu.VMEM((3, nx, ny, nz), f32), pltpu.SemaphoreType.DMA((4,))],
+        + [ints(tiles), ints(tiles), ints(nblocks), plan_copy]
+        + [pltpu.VMEM((3, nx, ny, nz), f32), pltpu.SemaphoreType.DMA((5,))],
         "ghost_contacts",
         contact_flops // 2,
-        places=[VMEM] * 3 + [SMEM],
-    )(tile_home, tile_partner, routes, below, above, before, after,
-      home_side, sums, state, cell_of, fluid)
+    )(tile_home, tile_partner, routes, plan, below, above, before, after,
+      home_side, sums, state, cell_of, spots, bounds, fluid)
 
     crossed = lax.all_to_all(
         outgoing.reshape(nbrick, 3 * chunk, width), "brick", split_axis=0, concat_axis=0, tiled=True
@@ -536,14 +701,14 @@
     crossed = crossed.reshape(nbrick * 3 * chunk, width)
 
     def places(count):
-        return [ints(count + GROUP)] * 2
-
-    block_flops = 16 * columns * nz * width
+        return [ints(4 * list_stride(count, cap))] * 2 + [ints(4)]
+
+    block_flops = 8 * columns * nz * width
     (started,) = call(
         functools.partial(first_deposit, nbrick, cap),
-        [struct(4 * columns, nz)],
+        [struct(8 * columns, nz // 2)],
         [VMEM],
-        places(nbrick * cap),
+        places(nbrick),
         "first_deposit",
         block_flops * nblocks // 3,
     )(crossed)
@@ -551,7 +716,7 @@
         functools.partial(advance, nbrick, cap),
         [
             struct(3, nx, ny, nz),
-            struct(3 * columns, 2 * nz, dtype=bf16),
+            struct(12 * columns, nz // 2, dtype=bf16),
             struct(nbrick * back, width),
             struct(nbrick * back, width),
         ],
@@ -559,10 +724,10 @@
         [
             pltpu.VMEM((2 * nbrick * chunk, width), f32),
             pltpu.VMEM((2 * nbrick * back, width), f32),
-            pltpu.VMEM((4 * columns, nz), f32),
+            pltpu.VMEM((8 * columns, nz // 2), f32),
         ]
         + [pltpu.VMEM((3, nx, ny, nz), f32)] * 2
-        + places(2 * nbrick * cap)
+        + places(2 * nbrick)
         + [pltpu.SemaphoreType.DMA((2,))],
         "advance",
         block_flops * nblocks,
@@ -574,7 +739,7 @@
         functools.partial(last_sample, nbrick, cap),
         [struct(nbrick * back, width)],
         [VMEM] * 2,
-        places(nbrick * cap),
+        places(nbrick),
         "last_sample",
         block_flops * nblocks // 4,
     )(crossed, table)
@@ -583,12 +748,13 @@
     )
     returned = lax.all_to_all(answers, "brick", split_axis=0, concat_axis=0, tiled=True)
     (velocity_next,) = call(
-        functools.partial(relax, cap),
+        functools.partial(relax, nbrick, cap),
         [struct(3, nblocks, width)],
-        [SMEM] + [VMEM] * 2,
-        [pltpu.VMEM((3, nblocks, width), f32)],
+        [SMEM, ANY] + [VMEM] * 3,
+        [pltpu.VMEM((3, nblocks, width), f32), chunk_tiles, plan_copy]
+        + [pltpu.SemaphoreType.DMA((1,))],
         "relax",
-    )(goals, updated, returned.reshape(nbrick * 3 * back, width))
+    )(routes, plan, updated, returned.reshape(nbrick * 3 * back, width), spots)
     return (jnp.transpose(velocity_next, (1, 0, 2)), fluid_next)
 
 

time: 91.8 us -> 90.2 us (0.983)
  Pallas kernels: 54.3 us -> 47.7 us
  blocking collectives: 17.5 us -> 22 us
    pallas_call x1, Pallas kernels: 29.6 us -> 13.2 us  [on_device(): call(functools.partial(advance, nbrick, cap), [struct(3, nx, ny, nz), str...]
    pallas_call x3, Pallas kernels: 14.8 us -> 20.3 us  [the longest x1 8.87 us: on_device(): call(functools.partial(own_contacts, codes, columns, nz), [struct((nblock...]
    pallas_call x1, Pallas kernels: 5.98 us -> 10.5 us  [on_device(): call(functools.partial(ghost_contacts, nbrick, cap, 4 * per), [struct(3,...]
    all_to_all x1, blocking collectives: 8.24 us -> 12.5 us  [on_device(): lax.all_to_all(answers, 'brick', split_axis=0, concat_axis=0, tiled=True)]
  transfers between devices with their start and end apart: 8 -> 8, of which waited for: 0 -> 0; matrix products, arithmetic and copies ran while one was open for 0% -> 0% of each run, Pallas kernels for 18% -> 17%
where the time goes in v2:
time: 90.2 us; the launch traced here: 90.8 us
  Pallas kernels  47.7 us (53%)
  blocking collectives  22 us (24%)
  starting transfers between devices  17.4 us (19%)
  local copies, waits for them, and re-layouts  1.82 us (2%)
  other arithmetic  1.02 us (1%)
    ppermute x8, starting transfers between devices, shifted(): lax.ppermute(x, axis, [(i, (i + step) % count) for i in range(count)])  17.4 us
    pallas_call x1, Pallas kernels, on_device(): call(functools.partial(advance, nbrick, cap), [struct(3, nx, ny, nz), str...  13.2 us
    all_to_all x1, blocking collectives, on_device(): lax.all_to_all(answers, 'brick', split_axis=0, concat_axis=0, tiled=True)  12.5 us
    pallas_call x1, Pallas kernels, on_device(): call(functools.partial(ghost_contacts, nbrick, cap, 4 * per), [struct(3,...  10.5 us
    all_to_all x1, blocking collectives, on_device(): lax.all_to_all(outgoing.reshape(nbrick, 3 * chunk, width), 'brick', split...  9.53 us
    pallas_call x1, Pallas kernels, on_device(): call(functools.partial(own_contacts, codes, columns, nz), [struct((nblock...  8.87 us
    pallas_call x1, Pallas kernels, on_device(): call(functools.partial(relax, nbrick, cap), [struct(3, nblocks, width)],...  7.9 us
    pallas_call x1, Pallas kernels, on_device(): call(functools.partial(first_deposit, nbrick, cap), [struct(8 * columns,...  3.49 us
  transfers between devices with their start and end apart: 8, of which 0 were waited for; matrix products, arithmetic and copies ran while one was open for 0% of the time, Pallas kernels for 17%

profile of v2, /device:TPU:0, one launch (start us, length us, event | category | flops | bytes accessed | tf_op | source)
XLA Modules:
  0.0 90.8 jit_solution(742566305119068457)
XLA Ops:
  0.7 1.0 %pad_maximum_fusion.1.state = f32[7,64,128]{2,1,0:T(8,128)S(1)} fusion(f32[3,64,128]{2,1,0:T(8,128)} %bitcast.26, f32[1,64,128]{2,1,0:T(8,128)} %bitcast.29, f32[3,64,128]{2,1,0:T(8,128)} %bitcast.27), kind=kLoop, calls=%fused_computation.1 | loop fusion | flops 114688 | bytes 458752 | tf_op jit(solution)/shard_map/concatenate | solution.py:642
  1.7 0.0 copy-start
  1.7 1.1 %copy-done = f32[3,4,32,512]{3,2,1,0:T(8,128)S(1)} copy-done((f32[3,4,32,512]{3,2,1,0:T(8,128)S(1)}, f32[3,4,32,512]{3,2,1,0:T(8,128)}, u32[]{:S(2)}) %copy-start) | copy-done | bytes 786456
  2.8 0.7 copy-done.4
  3.5 0.7 pack.1
  4.1 3.0 %collective-permute-start = (f32[440,128]{1,0:T(8,128)S(1)}, f32[440,128]{1,0:T(8,128)S(1)}, u32[]{:S(2)}, u32[]{:S(2)}) collective-permute-start(f32[440,128]{1,0:T(8,128)S(1)} %get-tuple-element.19), channel_id=1, source_target_pairs={{0,4},{4,8},{8,12},{12,16},{16,20},{20,24},{24,28},{28,0},{1,5},{5... | collective-permute-start | bytes 675848 | tf_op jit(solution)/shard_map/ppermute | solution.py:637
  7.2 3.1 %collective-permute-start.1 = (f32[440,128]{1,0:T(8,128)S(1)}, f32[440,128]{1,0:T(8,128)S(1)}, u32[]{:S(2)}, u32[]{:S(2)}) collective-permute-start(f32[440,128]{1,0:T(8,128)S(1)} %get-tuple-element.20), channel_id=1, source_target_pairs={{0,28},{4,0},{8,4},{12,8},{16,12},{20,16},{24,20},{28,24},{1,29},{... | collective-permute-start | bytes 675848 | tf_op jit(solution)/shard_map/ppermute | solution.py:637
  10.3 0.0 collective-permute-start.2
  10.3 1.7 %collective-permute-start.3 = (f32[104,128]{1,0:T(8,128)S(1)}, f32[104,128]{1,0:T(8,128)S(1)}, u32[]{:S(2)}, u32[]{:S(2)}) collective-permute-start(f32[104,128]{1,0:T(8,128)S(1)} %get-tuple-element.22), channel_id=1, source_target_pairs={{0,3},{1,0},{2,1},{3,2},{4,7},{5,4},{6,5},{7,6},{8,11},{9,8},{10,9... | collective-permute-start | bytes 159752 | tf_op jit(solution)/shard_map/ppermute | solution.py:637
  12.0 8.9 %own_contacts.1 = (f32[2080,128]{1,0:T(8,128)S(1)}, f32[1040,128]{1,0:T(8,128)S(1)}, f32[64,128]{1,0:T(8,128)S(1)}, s32[64,128]{1,0:T(8,128)S(1)}, f32[16,128]{1,0:T(8,128)S(1)}) custom-call(s32[128]{0:T(128)S(1)} %copy-done.5, s32[128]{0:T(128)S(1)} %copy-done.6, f32[7,64,128]{2,1,0:T(8,128)S(1)} %pad_maximum_fusion.1.state, s32[64,128]{1,0:T(8,128)S(1)} %copy-done.2, ...), custom_call_target="tpu_custom_call" | custom-call | flops 419430400 | bytes 1048576 | tf_op jit(solution)/shard_map/own_contacts/pallas_call | solution.py:667
  20.9 0.0 collective-permute-done.2.before
  20.9 0.0 collective-permute-done.3.after
  20.9 0.0 collective-permute-done.1.above
  20.9 10.5 %ghost_contacts.1 = (f32[3,64,128]{2,1,0:T(8,128)S(1)}, f32[672,128]{1,0:T(8,128)S(1)}, f32[3,4,32,512]{3,2,1,0:T(8,128)S(1)}) custom-call(s32[128]{0:T(128)S(1)} %copy-done.5, s32[128]{0:T(128)S(1)} %copy-done.6, s32[64]{0:T(128)S(1)} %bitcast.20, s32[64,128]{1,0:T(8,128)S(1)} %get-tuple-element.18.plan, f32[440,128]{1,0:T(8,128)S(1)} %collective-permute-done.below, ...), custom_call_target="tpu_custom_call" | custom-call | flops 209715200 | bytes 1048576 | tf_op jit(solution)/shard_map/ghost_contacts/pallas_call | solution.py:681
  31.5 9.5 %all_to_all.10 = f32[4,168,128]{2,1,0:T(8,128)S(1)} all-to-all(f32[4,168,128]{2,1,0:T(8,128)S(1)} %bitcast.17), channel_id=1, replica_groups=mesh['slab'=8,'brick'=4] {'brick'}, dimensions={0} | all-to-all | bytes 688128 | tf_op jit(solution)/shard_map/all_to_all | solution.py:696
  41.0 0.1 collective-permute-start.5
  41.1 4.7 %collective-permute-start.4 = (f32[4,56,128]{2,1,0:T(8,128)S(1)}, f32[4,56,128]{2,1,0:T(8,128)S(1)}, u32[]{:S(2)}, u32[]{:S(2)}) collective-permute-start(f32[4,56,128]{2,1,0:T(8,128)S(1)} %get-tuple-element.35), channel_id=1, source_target_pairs={{0,28},{4,0},{8,4},{12,8},{16,12},{20,16},{24,20},{28,24},{1,29},{... | collective-permute-start | bytes 344072 | tf_op jit(solution)/shard_map/ppermute | solution.py:637
  45.8 3.5 %first_deposit.1.start = f32[1024,256]{1,0:T(8,128)S(1)} custom-call(f32[672,128]{1,0:T(8,128)S(1)} %bitcast.15), custom_call_target="tpu_custom_call" | custom-call | flops 1431655808 | bytes 1048576 | tf_op jit(solution)/shard_map/first_deposit/pallas_call | solution.py:707
  49.3 13.2 %advance.1 = (f32[3,4,32,512]{3,2,1,0:T(8,128)}, bf16[1536,256]{1,0:T(8,128)(2,1)S(1)}, f32[160,128]{1,0:T(8,128)S(1)}, f32[160,128]{1,0:T(8,128)S(1)}) custom-call(f32[224,128]{1,0:T(8,128)S(1)} %bitcast.23, f32[224,128]{1,0:T(8,128)S(1)} %bitcast.22, f32[1024,256]{1,0:T(8,128)S(1)} %first_deposit.1.start, f32[3,4,32,512]{3,2,1,0:T(8,128)S(1)} %copy-done.1, ...), custom_call_target="tpu_custom_call" | custom-call | flops 4294967296 | bytes 1048576 | tf_op jit(solution)/shard_map/advance/pallas_call | solution.py:715
  62.6 0.1 collective-permute-start.6
  62.6 4.7 %collective-permute-start.7 = (f32[4,40,128]{2,1,0:T(8,128)S(1)}, f32[4,40,128]{2,1,0:T(8,128)S(1)}, u32[]{:S(2)}, u32[]{:S(2)}) collective-permute-start(f32[4,40,128]{2,1,0:T(8,128)S(1)} %bitcast.24), channel_id=1, source_target_pairs={{0,28},{4,0},{8,4},{12,8},{16,12},{20,16},{24,20},{28,24},{1,29},{... | collective-permute-start | bytes 245768 | tf_op jit(solution)/shard_map/ppermute | solution.py:637
  67.3 3.1 %last_sample.1 = f32[160,128]{1,0:T(8,128)S(1)} custom-call(f32[672,128]{1,0:T(8,128)S(1)} %bitcast.16, bf16[1536,256]{1,0:T(8,128)(2,1)S(1)} %get-tuple-element.31.table), custom_call_target="tpu_custom_call" | custom-call | flops 1073741824 | bytes 1048576 | tf_op jit(solution)/shard_map/last_sample/pallas_call | solution.py:738
  70.4 12.5 %all_to_all.11 = f32[4,120,128]{2,1,0:T(8,128)S(1)} all-to-all(f32[4,120,128]{2,1,0:T(8,128)S(1)} %pad_maximum_fusion), channel_id=1, replica_groups=mesh['slab'=8,'brick'=4] {'brick'}, dimensions={0} | all-to-all | bytes 491520 | tf_op jit(solution)/shard_map/all_to_all | solution.py:749
  82.9 7.9 %relax.1 = f32[3,64,128]{2,1,0:T(8,128)} custom-call(s32[64]{0:T(128)S(1)} %bitcast.21, s32[64,128]{1,0:T(8,128)S(1)} %get-tuple-element.18.plan, f32[3,64,128]{2,1,0:T(8,128)S(1)} %get-tuple-element.27.updated, f32[480,128]{1,0:T(8,128)S(1)} %bitcast.14, f32[64,128]{1,0:T(8,128)S(1)} %get-tuple-element.25.spots), custom_call_target="tpu_custom_call" | custom-call | bytes 1048576 | tf_op jit(solution)/shard_map/relax/pallas_call | solution.py:750
  (18 shorter events, 0.1 us)
Async XLA Ops:
  0.6 11.4 %copy-start.6 = (s32[128]{0:T(128)S(1)}, s32[128]{0:T(128)}, u32[]{:S(2)}) copy-start(s32[128]{0:T(128)} %partner_list.3) | copy-start | bytes 1540
  0.6 11.4 %copy-start.5 = (s32[128]{0:T(128)S(1)}, s32[128]{0:T(128)}, u32[]{:S(2)}) copy-start(s32[128]{0:T(128)} %home_list.3) | copy-start | bytes 1540
  0.7 11.4 %copy-start.2 = (s32[64,128]{1,0:T(8,128)S(1)}, s32[64,128]{1,0:T(8,128)}, u32[]{:S(2)}) copy-start(s32[64,128]{1,0:T(8,128)} %cell.3) | copy-start | bytes 98308
  0.7 11.4 %copy-start.3 = (s32[64,1]{0,1:T(1,128)S(1)}, s32[64,1]{0,1:T(1,128)}, u32[]{:S(2)}) copy-start(s32[64,1]{0,1:T(1,128)} %param.13) | copy-start | bytes 772
  1.7 1.1 %copy-start = (f32[3,4,32,512]{3,2,1,0:T(8,128)S(1)}, f32[3,4,32,512]{3,2,1,0:T(8,128)}, u32[]{:S(2)}) copy-start(f32[3,4,32,512]{3,2,1,0:T(8,128)} %fluid.5) | copy-start | bytes 2359300
  2.8 0.7 copy-start.4
  3.5 17.5 %copy-start.1 = (f32[3,4,32,512]{3,2,1,0:T(8,128)S(1)}, f32[3,4,32,512]{3,2,1,0:T(8,128)}, u32[]{:S(2)}) copy-start(f32[3,4,32,512]{3,2,1,0:T(8,128)} %fluid.5) | copy-start | bytes 2359300
  4.1 16.8 %collective-permute-start = (f32[440,128]{1,0:T(8,128)S(1)}, f32[440,128]{1,0:T(8,128)S(1)}, u32[]{:S(2)}, u32[]{:S(2)}) collective-permute-start(f32[440,128]{1,0:T(8,128)S(1)} %get-tuple-element.19), channel_id=1, source_target_pairs={{0,4},{4,8},{8,12},{12,16},{16,20},{20,24},{24,28},{28,0},{1,5},{5... | collective-permute-start | bytes 675848 | tf_op jit(solution)/shard_map/ppermute | solution.py:637
  7.2 13.8 %collective-permute-start.1 = (f32[440,128]{1,0:T(8,128)S(1)}, f32[440,128]{1,0:T(8,128)S(1)}, u32[]{:S(2)}, u32[]{:S(2)}) collective-permute-start(f32[440,128]{1,0:T(8,128)S(1)} %get-tuple-element.20), channel_id=1, source_target_pairs={{0,28},{4,0},{8,4},{12,8},{16,12},{20,16},{24,20},{28,24},{1,29},{... | collective-permute-start | bytes 675848 | tf_op jit(solution)/shard_map/ppermute | solution.py:637
  10.3 10.6 %collective-permute-start.2 = (f32[104,128]{1,0:T(8,128)S(1)}, f32[104,128]{1,0:T(8,128)S(1)}, u32[]{:S(2)}, u32[]{:S(2)}) collective-permute-start(f32[104,128]{1,0:T(8,128)S(1)} %get-tuple-element.21), channel_id=1, source_target_pairs={{0,1},{1,2},{2,3},{3,0},{4,5},{5,6},{6,7},{7,4},{8,9},{9,10},{10,1... | collective-permute-start | bytes 159752 | tf_op jit(solution)/shard_map/ppermute | solution.py:637
  10.3 10.6 %collective-permute-start.3 = (f32[104,128]{1,0:T(8,128)S(1)}, f32[104,128]{1,0:T(8,128)S(1)}, u32[]{:S(2)}, u32[]{:S(2)}) collective-permute-start(f32[104,128]{1,0:T(8,128)S(1)} %get-tuple-element.22), channel_id=1, source_target_pairs={{0,3},{1,0},{2,1},{3,2},{4,7},{5,4},{6,5},{7,6},{8,11},{9,8},{10,9... | collective-permute-start | bytes 159752 | tf_op jit(solution)/shard_map/ppermute | solution.py:637
  41.0 8.3 %collective-permute-start.5 = (f32[4,56,128]{2,1,0:T(8,128)S(1)}, f32[4,56,128]{2,1,0:T(8,128)S(1)}, u32[]{:S(2)}, u32[]{:S(2)}) collective-permute-start(f32[4,56,128]{2,1,0:T(8,128)S(1)} %get-tuple-element.34), channel_id=1, source_target_pairs={{0,4},{4,8},{8,12},{12,16},{16,20},{20,24},{24,28},{28,0},{1,5},{5... | collective-permute-start | bytes 344072 | tf_op jit(solution)/shard_map/ppermute | solution.py:637
  41.1 8.2 %collective-permute-start.4 = (f32[4,56,128]{2,1,0:T(8,128)S(1)}, f32[4,56,128]{2,1,0:T(8,128)S(1)}, u32[]{:S(2)}, u32[]{:S(2)}) collective-permute-start(f32[4,56,128]{2,1,0:T(8,128)S(1)} %get-tuple-element.35), channel_id=1, source_target_pairs={{0,28},{4,0},{8,4},{12,8},{16,12},{20,16},{24,20},{28,24},{1,29},{... | collective-permute-start | bytes 344072 | tf_op jit(solution)/shard_map/ppermute | solution.py:637
  62.6 7.8 %collective-permute-start.6 = (f32[4,40,128]{2,1,0:T(8,128)S(1)}, f32[4,40,128]{2,1,0:T(8,128)S(1)}, u32[]{:S(2)}, u32[]{:S(2)}) collective-permute-start(f32[4,40,128]{2,1,0:T(8,128)S(1)} %bitcast.25), channel_id=1, source_target_pairs={{0,4},{4,8},{8,12},{12,16},{16,20},{20,24},{24,28},{28,0},{1,5},{5... | collective-permute-start | bytes 245768 | tf_op jit(solution)/shard_map/ppermute | solution.py:637
  62.6 7.8 %collective-permute-start.7 = (f32[4,40,128]{2,1,0:T(8,128)S(1)}, f32[4,40,128]{2,1,0:T(8,128)S(1)}, u32[]{:S(2)}, u32[]{:S(2)}) collective-permute-start(f32[4,40,128]{2,1,0:T(8,128)S(1)} %bitcast.24), channel_id=1, source_target_pairs={{0,28},{4,0},{8,4},{12,8},{16,12},{20,16},{24,20},{28,24},{1,29},{... | collective-permute-start | bytes 245768 | tf_op jit(solution)/shard_map/ppermute | solution.py:637
